TPU v7x, 256 devices: a whole 4x4x8 slice. The times are simulated.
256 devices in a mesh: tile: 32 (over y_hi, z, core), sub: 2 (over y_lo), rep: 4 (over x).
Axes of the slice: x: 4, y: 4 (y_hi: 2, y_lo: 2; y = y_hi * 2 + y_lo), z: 8, core: 2. Of those that a mesh axis runs over, the one named last changes fastest.
Arguments:
- initial_state: bfloat16 [24, 64, 64, 128], P('rep', ('tile', 'sub')), parts along dimension 0, may hold values from -6 to 6
- state_tangent: bfloat16 [24, 64, 64, 128], P('rep', ('tile', 'sub')), parts along dimension 0, may hold values from -6 to 6
- cotangent: bfloat16 [24, 64, 64, 128], P('rep', ('tile', 'sub')), parts along dimension 0, may hold values from -6 to 6
- weight_first: bfloat16 [9, 128, 128], replicated, may hold values from -0.1875 to 0.1875
- weight_second: bfloat16 [9, 128, 128], replicated, may hold values from -0.1875 to 0.1875
- tangent_first: bfloat16 [9, 128, 128], replicated, may hold values from -0.1875 to 0.1875
- tangent_second: bfloat16 [9, 128, 128], replicated, may hold values from -0.1875 to 0.1875
- neighbour: int32 [6, 4], replicated, may hold values from 0 to 23, as said below
Outputs:
- next_state: bfloat16 [24, 64, 64, 128], P('rep', ('tile', 'sub')), parts along dimension 0
- adjoint: bfloat16 [24, 64, 64, 128], P('rep', ('tile', 'sub')), parts along dimension 0
- adjoint_tangent: bfloat16 [24, 64, 64, 128], P('rep', ('tile', 'sub')), parts along dimension 0
- weight_gradient: float32 [8, 9, 128, 128], P('rep'), parts along dimension 0
- hessian_product: float32 [8, 9, 128, 128], P('rep'), parts along dimension 0
There are 4 independent parts, one for each index of `rep`. A program takes and returns all parts, laid end to end along the dimension named above; an argument that names none is the same for every part. Nothing has to cross between parts.
Inputs may be any that keep to these rules, and one draw needn't show every extreme that they name: neighbour[f, s] = 4 g + t means that side s of face f meets side t of face g; the relation is symmetric, each value appears once, no face meets itself, and the six faces close into the surface of a cube, every face seen from outside.
All inputs are finite; a program needn't handle non-finite values.
Results may differ from a plain program's by a relative error of at most 0.0049.
Values may be sent and summed in bfloat16 or wider, within the bound.
A program may use at most 128 MiB of HBM per device.

v0:
```python
import jax
import jax.numpy as jnp
from jax import lax
from jax.sharding import PartitionSpec as P

step_size = 0.5


def broadcast(block, axis, source):
    block = jnp.where(lax.axis_index(axis) == source, block, jnp.zeros_like(block))
    return lax.psum(block, axis)


def extended(cells, sides, width):
    for axis, dim in sides:
        count = lax.axis_size(axis)
        ends = count - 1
        head = lax.slice_in_dim(cells, 0, width, axis=dim)
        tail = lax.slice_in_dim(cells, cells.shape[dim] - width, cells.shape[dim], axis=dim)
        cells = jnp.concatenate(
            [
                lax.ppermute(tail, axis, [(i, (i + 1) % count) for i in range(ends)]),
                cells,
                lax.ppermute(head, axis, [((i + 1) % count, i) for i in range(ends)]),
            ],
            axis=dim,
        )
    return cells


def side_tables(neighbour):
    source = neighbour.reshape(24)
    picker = (source[:, None] == jnp.arange(24, dtype=jnp.int32)[None, :]).astype(jnp.bfloat16)
    own_side = jnp.tile(jnp.arange(4, dtype=jnp.int32), 6)
    other_side = source % 4
    flipped = (own_side < 2) == (other_side < 2)
    offsets = jnp.arange(3, dtype=jnp.int32)[None, :] - 1
    along_sign = jnp.where(flipped[:, None], -offsets, offsets)
    other_col = other_side[:, None]
    row_tap = jnp.where(other_col == 0, 0, jnp.where(other_col == 2, 2, 1 - along_sign))
    col_tap = jnp.where(other_col == 1, 2, jnp.where(other_col == 3, 0, 1 - along_sign))
    chosen = 3 * row_tap + col_tap
    selector = (chosen[:, :, None] == jnp.arange(9, dtype=jnp.int32)[None, None, :]).astype(
        jnp.bfloat16
    )
    return (picker, flipped, selector)


def face_halo(fields, picker, flipped):
    device_count = lax.axis_size(("tile", "sub"))
    position = lax.axis_index(("tile", "sub"))
    stacked = fields.shape[0]
    height = fields.shape[2]
    face_width = fields.shape[3]
    channels = fields.shape[4]
    side_rims = jnp.stack([fields[:, :, :, face_width - 1], fields[:, :, :, 0]], axis=2)
    columns = lax.all_gather(side_rims, ("tile", "sub"), axis=3, tiled=True)
    upper_rims = broadcast(fields[:, :, 0], ("tile", "sub"), 0)
    lower_rims = broadcast(fields[:, :, height - 1], ("tile", "sub"), device_count - 1)
    edge_table = jnp.stack([upper_rims, columns[:, :, 0], lower_rims, columns[:, :, 1]], axis=2)
    flat_edges = edge_table.reshape(stacked, 24, face_width, channels)
    margins = jnp.einsum(
        "ab,kbwc->kawc", picker, flat_edges, preferred_element_type=jnp.float32
    ).astype(jnp.bfloat16)
    margins = jnp.where(flipped[None, :, None, None], margins[:, :, ::-1], margins)
    margins = margins.reshape(stacked, 6, 4, face_width, channels)
    row_start = position * height
    left_margin = lax.dynamic_slice_in_dim(margins[:, :, 3], row_start, height, 2)
    right_margin = lax.dynamic_slice_in_dim(margins[:, :, 1], row_start, height, 2)
    middle = jnp.concatenate(
        [left_margin[:, :, :, None], fields, right_margin[:, :, :, None]], axis=3
    )
    padded = extended(middle, ((("tile", "sub"), 2),), 1)
    upper_row = jnp.pad(margins[:, :, 0], ((0, 0), (0, 0), (1, 1), (0, 0)))
    lower_row = jnp.pad(margins[:, :, 2], ((0, 0), (0, 0), (1, 1), (0, 0)))
    first_row = jnp.where(position == 0, upper_row, padded[:, :, 0])
    last_row = jnp.where(position == device_count - 1, lower_row, padded[:, :, height + 1])
    return jnp.concatenate(
        [first_row[:, :, None], padded[:, :, 1 : height + 1], last_row[:, :, None]], axis=2
    )


def forward_taps(padded):
    height = padded.shape[1] - 2
    face_width = padded.shape[2] - 2
    windows = [
        padded[:, tap_row : tap_row + height, tap_col : tap_col + face_width]
        for tap_row in range(3)
        for tap_col in range(3)
    ]
    return jnp.concatenate(windows, axis=-1)


def inner_taps(padded, position, device_count):
    height = padded.shape[1] - 2
    face_width = padded.shape[2] - 2
    row_ids = jnp.arange(height + 2)
    col_ids = jnp.arange(face_width + 2)
    keep_rows = ((row_ids > 0) | (position > 0)) & (
        (row_ids < height + 1) | (position < device_count - 1)
    )
    keep_cols = (col_ids > 0) & (col_ids < face_width + 1)
    keep_cells = keep_rows[:, None] & keep_cols[None, :]
    masked = jnp.where(keep_cells[None, :, :, None], padded, jnp.zeros((), padded.dtype))
    windows = [
        masked[:, 2 - tap_row : 2 - tap_row + height, 2 - tap_col : 2 - tap_col + face_width]
        for tap_row in range(3)
        for tap_col in range(3)
    ]
    return jnp.concatenate(windows, axis=-1)


def transposed(kernel):
    return kernel.transpose(0, 2, 1).reshape(9 * kernel.shape[2], kernel.shape[1])


def select_kernel(selector, kernel):
    return jnp.einsum("xdk,kio->xdio", selector, kernel, preferred_element_type=jnp.float32).astype(
        jnp.bfloat16
    )


def add_sides(inner, padded, position, device_count, chosen):
    height = inner.shape[1]
    face_width = inner.shape[2]
    kernels = chosen.reshape(6, 4, 3, chosen.shape[2], chosen.shape[3])

    def along_line(margin_line, length, side_number):
        total_term = jnp.zeros((margin_line.shape[0], length, chosen.shape[2]), jnp.float32)
        for offset in range(3):
            total_term = total_term + jnp.einsum(
                "flo,fio->fli",
                margin_line[:, offset : offset + length],
                kernels[:, side_number, offset],
                preferred_element_type=jnp.float32,
            )
        return total_term

    upper_term = along_line(padded[:, 0], face_width, 0)
    right_term = along_line(padded[:, :, face_width + 1], height, 1)
    lower_term = along_line(padded[:, height + 1], face_width, 2)
    left_term = along_line(padded[:, :, 0], height, 3)
    result = inner.at[:, :, face_width - 1].add(right_term).at[:, :, 0].add(left_term)
    result = result.at[:, 0].add(jnp.where(position == 0, upper_term, 0.0))
    result = result.at[:, height - 1].add(jnp.where(position == device_count - 1, lower_term, 0.0))
    return result


def weight_term(tap_stack, gradient):
    channels = gradient.shape[-1]
    return jnp.einsum(
        "frjk,frjd->kd", tap_stack, gradient, preferred_element_type=jnp.float32
    ).reshape(9, channels, channels)


def on_device(
    initial_state,
    state_tangent,
    cotangent,
    weight_first,
    weight_second,
    tangent_first,
    tangent_second,
    neighbour,
):
    picker, flipped, selector = side_tables(neighbour)
    device_count = lax.axis_size(("tile", "sub"))
    position = lax.axis_index(("tile", "sub"))
    channels = initial_state.shape[3]
    face_width = initial_state.shape[2]
    first_flat = weight_first.reshape(9 * channels, channels)
    second_flat = weight_second.reshape(9 * channels, channels)
    inputs = face_halo(jnp.stack([initial_state, state_tangent]), picker, flipped)
    taps_state = forward_taps(inputs[0])
    taps_tangent = forward_taps(inputs[1])
    joined = jnp.einsum(
        "frjk,kd->frjd",
        taps_state,
        jnp.concatenate([first_flat, tangent_first.reshape(9 * channels, channels)], axis=1),
        preferred_element_type=jnp.float32,
    )
    hidden = joined[..., :channels]
    hidden_tangent = joined[..., channels:] + jnp.einsum(
        "frjk,kd->frjd", taps_tangent, first_flat, preferred_element_type=jnp.float32
    )
    squash = jnp.tanh(hidden)
    derivative = 1.0 - squash * squash
    activated = squash.astype(jnp.bfloat16)
    activated_tangent = (derivative * hidden_tangent).astype(jnp.bfloat16)
    layer_two = face_halo(jnp.stack([activated, activated_tangent]), picker, flipped)
    taps_act = forward_taps(layer_two[0])
    taps_act_tangent = forward_taps(layer_two[1])
    change = jnp.einsum("frjk,kd->frjd", taps_act, second_flat, preferred_element_type=jnp.float32)
    next_state = (initial_state.astype(jnp.float32) + step_size * change).astype(jnp.bfloat16)
    seed_field = (step_size * cotangent.astype(jnp.float32)).astype(jnp.bfloat16)
    grad_second = weight_term(taps_act, seed_field)
    curve_second = weight_term(taps_act_tangent, seed_field)
    seed_padded = face_halo(seed_field[None], picker, flipped)[0]
    seed_taps = inner_taps(seed_padded, position, device_count)
    seed_inner = jnp.einsum(
        "frjk,kc->frjc",
        seed_taps,
        jnp.concatenate([transposed(weight_second), transposed(tangent_second)], axis=1),
        preferred_element_type=jnp.float32,
    )
    backward = add_sides(
        seed_inner[..., :channels],
        seed_padded,
        position,
        device_count,
        select_kernel(selector, weight_second),
    )
    backward_tangent = add_sides(
        seed_inner[..., channels:],
        seed_padded,
        position,
        device_count,
        select_kernel(selector, tangent_second),
    )
    delta_field = (derivative * backward).astype(jnp.bfloat16)
    delta_tangent = (
        derivative * backward_tangent - 2.0 * squash * derivative * hidden_tangent * backward
    ).astype(jnp.bfloat16)
    grad_first = weight_term(taps_state, delta_field)
    curve_first = weight_term(taps_tangent, delta_field) + weight_term(taps_state, delta_tangent)
    deltas = face_halo(jnp.stack([delta_field, delta_tangent]), picker, flipped)
    delta_taps = inner_taps(deltas[0], position, device_count)
    tangent_taps = inner_taps(deltas[1], position, device_count)
    first_back = transposed(weight_first)
    paired = jnp.einsum(
        "frjk,kc->frjc",
        delta_taps,
        jnp.concatenate([first_back, transposed(tangent_first)], axis=1),
        preferred_element_type=jnp.float32,
    )
    own_first = select_kernel(selector, weight_first)
    adjoint_inner = add_sides(paired[..., :channels], deltas[0], position, device_count, own_first)
    tangent_inner = paired[..., channels:] + jnp.einsum(
        "frjk,kc->frjc", tangent_taps, first_back, preferred_element_type=jnp.float32
    )
    tangent_inner = add_sides(tangent_inner, deltas[1], position, device_count, own_first)
    tangent_inner = add_sides(
        tangent_inner, deltas[0], position, device_count, select_kernel(selector, tangent_first)
    )
    adjoint = (cotangent.astype(jnp.float32) + adjoint_inner).astype(jnp.bfloat16)
    adjoint_tangent = tangent_inner.astype(jnp.bfloat16)
    grad_first, grad_second, curve_first, curve_second = lax.psum(
        (grad_first, grad_second, curve_first, curve_second), ("tile", "sub")
    )
    weight_gradient = jnp.stack([grad_first, grad_second]) / face_width
    hessian_product = jnp.stack([curve_first, curve_second]) / face_width
    return (next_state, adjoint, adjoint_tangent, weight_gradient, hessian_product)


def solution(mesh):
    placed = (
        P("rep", ("tile", "sub"), None, None),
        P("rep", ("tile", "sub"), None, None),
        P("rep", ("tile", "sub"), None, None),
        P(),
        P(),
        P(),
        P(),
        P(),
    )
    return jax.shard_map(
        on_device,
        mesh=mesh,
        in_specs=placed,
        out_specs=(
            P("rep", ("tile", "sub"), None, None),
            P("rep", ("tile", "sub"), None, None),
            P("rep", ("tile", "sub"), None, None),
            P("rep", None, None, None),
            P("rep", None, None, None),
        ),
        check_vma=False,
    )
```

profile of v0, /device:TPU:1, one launch (start us, length us, event | category | flops | bytes accessed | tf_op | source)
XLA Modules:
  0.0 1033.6 jit_solution(2591001838433969738)
XLA Ops:
  10.9 129.0 %all_gather.14 = bf16[1,6,2,64,128]{4,2,1,0,3:T(2,128)(2,1)S(1)} all-gather(bf16[1,6,2,1,128]{4,2,1,0,3:T(2,128)(2,1)S(1)} %copy.201), channel_id=1, replica_groups=mesh['tile'=32,'sub'=2,'rep'=4] {'tile','sub'}, dimensions={3}, use_global_device_ids=true | all-gather | bytes 199680 | tf_op jit(solution)/shard_map/all_gather | solution.py:57
  142.8 5.6 fusion.241
  149.3 4.8 fusion.240
  155.9 123.5 %all_gather.12 = bf16[2,6,2,64,128]{4,2,1,0,3:T(2,128)(2,1)S(1)} all-gather(bf16[2,6,2,1,128]{4,2,1,0,3:T(2,128)(2,1)S(1)} %copy.180), channel_id=1, replica_groups=mesh['tile'=32,'sub'=2,'rep'=4] {'tile','sub'}, dimensions={3}, use_global_device_ids=true | all-gather | bytes 399360 | tf_op jit(solution)/shard_map/all_gather | solution.py:57
  282.3 5.7 fusion.238
  288.8 4.8 fusion.239
  297.4 2.8 collective-permute-start.4
  300.3 6.3 collective-permute-start.5
  312.0 3.9 collective-permute-start.1
  326.9 1.9 fusion.108
  346.9 123.6 %all_gather.13 = bf16[2,6,2,64,128]{4,2,1,0,3:T(2,128)(2,1)S(1)} all-gather(bf16[2,6,2,1,128]{4,2,1,0,3:T(2,128)(2,1)S(1)} %copy.191), channel_id=1, replica_groups=mesh['tile'=32,'sub'=2,'rep'=4] {'tile','sub'}, dimensions={3}, use_global_device_ids=true | all-gather | bytes 399360 | tf_op jit(solution)/shard_map/all_gather | solution.py:57
  471.8 123.9 %all_gather.15 = bf16[2,6,2,64,128]{4,2,1,0,3:T(2,128)(2,1)S(1)} all-gather(bf16[2,6,2,1,128]{4,2,1,0,3:T(2,128)(2,1)S(1)} %copy.240), channel_id=1, replica_groups=mesh['tile'=32,'sub'=2,'rep'=4] {'tile','sub'}, dimensions={3}, use_global_device_ids=true | all-gather | bytes 399360 | tf_op jit(solution)/shard_map/all_gather | solution.py:57
  597.3 2.4 fusion.4
  601.0 177.0 %all-reduce.17.cloned.1.call-done = (bf16[2,6,1,64,128]{4,3,1,0,2:T(8,128)(2,1)}, bf16[2,6,1,64,128]{4,3,1,0,2:T(8,128)(2,1)}, bf16[2,6,1,64,128]{4,3,1,0,2:T(8,128)(2,1)}, bf16[2,6,1,64,128]{4,3,1,0,2:T(8,128)(2,1)}) async-done(((bf16[2,6,1,64,128]{4,3,1,0,2:T(8,128)(2,1)}, bf16[2,6,1,64,128]{4,3,1,0,2:T(8,128)(2,1)}, bf16[2,6,1,64,128]{4,3,1,0,2:T(8,128)(2,1)}, bf16[2,6,1,64,128]{4,3,1,0,2:T(8,128)(2,1)}), ...) | async-done | bytes 786448 | tf_op jit(solution)/shard_map/psum | solution.py:11
  783.9 3.0 collective-permute-start.6
  787.0 3.0 collective-permute-start.2
  790.0 2.6 collective-permute-start.3
  792.7 3.9 collective-permute-start.7
  796.9 9.4 collective-permute-done.7
  812.7 2.0 fusion.92
  814.7 2.0 fusion.145
  816.7 2.0 fusion.126
  840.7 182.5 %all-reduce.15.cloned.1.call-done = (f32[1,9,128,128]{3,2,1,0:T(8,128)}, f32[1,9,128,128]{3,2,1,0:T(8,128)}, f32[1,9,128,128]{3,2,1,0:T(8,128)}, f32[1,9,128,128]{3,2,1,0:T(8,128)}) async-done(((f32[1,9,128,128]{3,2,1,0:T(8,128)}, f32[1,9,128,128]{3,2,1,0:T(8,128)}, f32[1,9,128,128]{3,2,1,0:T(8,128)}, f32[1,9,128,128]{3,2,1,0:T(8,128)}), (f32[1,9,128,128]{3,2,1,0:T(8,128)}, f32[1,9,128,128]{3,2,1,0:T(8,128)}, ...) | async-done | bytes 2359312 | tf_op jit(solution)/shard_map/psum | solution.py:247
  1023.3 2.5 maximum_multiply_fusion.1
  (457 shorter events, 89.3 us)
Async XLA Ops:
  7.2 288.3 %all-reduce.19.cloned.1.call-start = ((), (), s32[]{:S(2)}) async-start(), calls=%async_computation.2 | async-start | bytes 1179648 | tf_op jit(solution)/shard_map/psum | solution.py:11
  10.7 130.9 %copy-start.80 = (s32[6,4]{0,1:T(4,128)S(1)}, s32[6,4]{0,1:T(4,128)}, u32[]{:S(2)}) copy-start(s32[6,4]{0,1:T(4,128)} %param.55) | copy-start | bytes 292
  10.7 131.3 %copy-start.2 = (bf16[9,128,128]{2,1,0:T(8,128)(2,1)S(1)}, bf16[9,128,128]{2,1,0:T(8,128)(2,1)}, u32[]{:S(2)}) copy-start(bf16[9,128,128]{2,1,0:T(8,128)(2,1)} %param.54) | copy-start | bytes 884740
  10.7 767.3 %all-reduce.17.cloned.1.call-start = ((), (), s32[]{:S(2)}) async-start(), calls=%async_computation.1 | async-start | bytes 1572864 | tf_op jit(solution)/shard_map/psum | solution.py:11
  297.0 9.5 copy-start.62
  297.0 9.5 copy-start.63
  297.0 9.5 copy-start.74
  297.0 9.5 copy-start.75
  297.4 19.4 %collective-permute-start.4 = (bf16[1,6,1,66,128]{4,3,1,2,0:T(8,128)(2,1)S(1)}, bf16[1,6,1,66,128]{4,3,1,2,0:T(8,128)(2,1)S(1)}, u32[]{:S(2)}, u32[]{:S(2)}) collective-permute-start(bf16[1,6,1,66,128]{4,3,1,2,0:T(8,128)(2,1)S(1)} %pad_maximum_fusion.13), channel_id=1, source_target_pairs={{0,4},{4,8},{8,12},{12,16},{16,20},{20,24},{24,28},{28,32},{32,36}... | collective-permute-start | bytes 304136 | tf_op jit(solution)/shard_map/ppermute | solution.py:22
  300.3 16.7 %collective-permute-start.5 = (bf16[1,6,1,66,128]{4,3,1,2,0:T(8,128)(2,1)S(1)}, bf16[1,6,1,66,128]{4,3,1,2,0:T(8,128)(2,1)S(1)}, u32[]{:S(2)}, u32[]{:S(2)}) collective-permute-start(bf16[1,6,1,66,128]{4,3,1,2,0:T(8,128)(2,1)S(1)} %pad_maximum_fusion.13), channel_id=1, source_target_pairs={{4,0},{8,4},{12,8},{16,12},{20,16},{24,20},{28,24},{32,28},{36,32}... | collective-permute-start | bytes 304136 | tf_op jit(solution)/shard_map/ppermute | solution.py:24
  310.1 29.5 %collective-permute-start = (bf16[2,6,1,66,128]{4,3,1,0,2:T(8,128)(2,1)}, bf16[2,6,1,66,128]{4,3,1,0,2:T(8,128)(2,1)}, u32[]{:S(2)}, u32[]{:S(2)}) collective-permute-start(bf16[2,6,1,66,128]{4,3,1,0,2:T(8,128)(2,1)} %get-tuple-element.376), channel_id=1, source_target_pairs={{0,4},{4,8},{8,12},{12,16},{16,20},{20,24},{24,28},{28,32},{32,36}... | collective-permute-start | bytes 608264 | tf_op jit(solution)/shard_map/ppermute | solution.py:22
  312.0 28.7 %collective-permute-start.1 = (bf16[2,6,1,66,128]{4,3,1,0,2:T(8,128)(2,1)}, bf16[2,6,1,66,128]{4,3,1,0,2:T(8,128)(2,1)}, u32[]{:S(2)}, u32[]{:S(2)}) collective-permute-start(bf16[2,6,1,66,128]{4,3,1,0,2:T(8,128)(2,1)} %get-tuple-element.376), channel_id=1, source_target_pairs={{4,0},{8,4},{12,8},{16,12},{20,16},{24,20},{28,24},{32,28},{36,32}... | collective-permute-start | bytes 608264 | tf_op jit(solution)/shard_map/ppermute | solution.py:24
  329.0 6.4 copy-start.41
  597.1 426.2 %all-reduce.15.cloned.1.call-start = ((), (), s32[]{:S(2)}) async-start(), calls=%async_computation | async-start | bytes 4718592 | tf_op jit(solution)/shard_map/psum | solution.py:247
  599.7 178.2 %copy-start.64 = (bf16[2,6,1,64,128]{4,3,1,0,2:T(8,128)(2,1)S(1)}, bf16[2,6,1,64,128]{4,3,1,0,2:T(8,128)(2,1)}, u32[]{:S(2)}) copy-start(bf16[2,6,1,64,128]{4,3,1,0,2:T(8,128)(2,1)} %copy.399) | copy-start | bytes 589828
  783.9 12.9 %collective-permute-start.6 = (bf16[2,6,1,66,128]{4,3,1,2,0:T(8,128)(2,1)S(1)}, bf16[2,6,1,66,128]{4,3,1,2,0:T(8,128)(2,1)S(1)}, u32[]{:S(2)}, u32[]{:S(2)}) collective-permute-start(bf16[2,6,1,66,128]{4,3,1,2,0:T(8,128)(2,1)S(1)} %get-tuple-element.374), channel_id=1, source_target_pairs={{0,4},{4,8},{8,12},{12,16},{16,20},{20,24},{24,28},{28,32},{32,36}... | collective-permute-start | bytes 608264 | tf_op jit(solution)/shard_map/ppermute | solution.py:22
  787.0 20.5 %collective-permute-start.2 = (bf16[2,6,1,66,128]{4,3,1,0,2:T(8,128)(2,1)S(1)}, bf16[2,6,1,66,128]{4,3,1,0,2:T(8,128)(2,1)S(1)}, u32[]{:S(2)}, u32[]{:S(2)}) collective-permute-start(bf16[2,6,1,66,128]{4,3,1,0,2:T(8,128)(2,1)S(1)} %pad_maximum_fusion.11), channel_id=1, source_target_pairs={{0,4},{4,8},{8,12},{12,16},{16,20},{20,24},{24,28},{28,32},{32,36}... | collective-permute-start | bytes 608264 | tf_op jit(solution)/shard_map/ppermute | solution.py:22
  790.0 17.6 %collective-permute-start.3 = (bf16[2,6,1,66,128]{4,3,1,0,2:T(8,128)(2,1)S(1)}, bf16[2,6,1,66,128]{4,3,1,0,2:T(8,128)(2,1)S(1)}, u32[]{:S(2)}, u32[]{:S(2)}) collective-permute-start(bf16[2,6,1,66,128]{4,3,1,0,2:T(8,128)(2,1)S(1)} %pad_maximum_fusion.11), channel_id=1, source_target_pairs={{4,0},{8,4},{12,8},{16,12},{20,16},{24,20},{28,24},{32,28},{36,32}... | collective-permute-start | bytes 608264 | tf_op jit(solution)/shard_map/ppermute | solution.py:24
  792.7 13.7 %collective-permute-start.7 = (bf16[2,6,1,66,128]{4,3,1,2,0:T(8,128)(2,1)S(1)}, bf16[2,6,1,66,128]{4,3,1,2,0:T(8,128)(2,1)S(1)}, u32[]{:S(2)}, u32[]{:S(2)}) collective-permute-start(bf16[2,6,1,66,128]{4,3,1,2,0:T(8,128)(2,1)S(1)} %get-tuple-element.374), channel_id=1, source_target_pairs={{4,0},{8,4},{12,8},{16,12},{20,16},{24,20},{28,24},{32,28},{36,32}... | collective-permute-start | bytes 608264 | tf_op jit(solution)/shard_map/ppermute | solution.py:24
  812.6 6.3 copy-start.6
  812.6 6.9 copy-start.5
  812.6 6.1 copy-start.26
  812.6 6.7 copy-start.25
  812.7 7.3 copy-start.24
  (69 other events, 158.4 us)
Sparse Core Ops, SparseCore 0:
  12.4 185.0 all-reduce.18
  597.2 180.7 all-reduce.16
  833.2 190.0 all-reduce.14
where the time goes:
time: 1040 us; the launch traced here: 1030 us
  blocking collectives  500 us (48%)
  waiting for transfers between devices  369 us (35%)
  local copies, waits for them, and re-layouts  54.9 us (5%)
  matrix products  47.7 us (5%)
  starting transfers between devices  27.8 us (3%)
  other arithmetic  18.1 us (2%)
  between operations  16 us (2%)
    all_gather x4, blocking collectives, face_halo(): columns = lax.all_gather(side_rims, ('tile', 'sub'), axis=3, tiled=True)  500 us
    psum x1, waiting for transfers between devices, on_device(): lax.psum((grad_first, grad_second, curve_first, curve_second), ('tile', '...  183 us
    psum x2, waiting for transfers between devices, broadcast(): return lax.psum(block, axis)  177 us
    dot_general x60, matrix products, along_line(): jnp.einsum('flo,fio->fli', margin_line[:, offset:offset + length], kernel...  31.8 us
    slice x4, local copies, waits for them, and re-layouts, along_line(): kernels[:, side_number, offset]  21 us
  transfers between devices with their start and end apart: 11, of which 3 were waited for; matrix products, arithmetic and copies ran while one was open for 7% of the time, Pallas kernels for 0%

commit v1 on v0

v1 whole, which is shorter than its diff:
```python
import functools

import jax
import jax.numpy as jnp
from jax import lax
from jax.experimental import pallas as pl
from jax.experimental.pallas import tpu as pltpu
from jax.sharding import PartitionSpec as P

MESH = pl.DeviceIdType.MESH
BF = jnp.bfloat16
F32 = jnp.float32
C = 128
K9 = 9 * C
SIDES = 16


def dot(a, b):
    return jnp.dot(a, b, preferred_element_type=F32)


def dot_t(a, b):
    return lax.dot_general(a, b, (((0,), (0,)), ((), ())), preferred_element_type=F32)


def iota(shape, dim):
    return lax.broadcasted_iota(jnp.int32, shape, dim)


def onehot(mask):
    return jnp.where(mask, 1.0, 0.0).astype(BF)


def kernel(
    n,
    ny,
    nz,
    u_ref,
    v_ref,
    c_ref,
    w1_ref,
    w2_ref,
    t1_ref,
    t2_ref,
    nb_ref,
    next_ref,
    adj_ref,
    adt_ref,
    out_ref,
    rb,
    mb,
    ebuf,
    hm,
    zs,
    rx,
    mt,
    sel,
    selh,
    amat,
    bmat,
    c0mat,
    c2mat,
    wraw,
    wf1,
    ws1,
    ws2,
    padf,
    padz,
    tu,
    tv,
    ts,
    tx,
    ty,
    sq,
    aext,
    dd,
    field,
    gsum,
    gs,
    gr,
    yf,
    ys,
    yr,
    zf,
    zst,
    zr,
    lsem,
    bulk_s,
    bulk_r,
    e_s,
    e_r,
    hm_s,
    rx_r,
    z_s,
    z_r,
    mt_s,
    mt_r,
    c_s,
    c_r,
    y_s,
    y_r,
    zz_s,
    zz_r,
    gz_s,
    gz_r,
    gy_s,
    gy_r,
    gc_s,
    gc_r,
):
    F = n
    cells = 6 * F
    rep = lax.axis_index("rep")
    r = lax.axis_index("tile") * 2 + lax.axis_index("sub")
    core = lax.rem(lax.div(r, 2), 2)
    z = lax.rem(lax.div(r, 4), nz)
    yhi = lax.div(r, 4 * nz)
    ylo = lax.rem(r, 2)
    y = yhi * 2 + ylo

    def dev(p):
        return (lax.div(p, 2), lax.rem(p, 2), rep)

    def make(hi, zc, co, lo):
        return ((hi * nz + zc) * 2 + co) * 2 + lo

    up = lax.rem(r + n - 1, n)
    dn = lax.rem(r + 1, n)
    mirror = n - 1 - r
    partner = make(yhi, z, 1 - core, ylo)

    def ypeer(d):
        q = lax.rem(y + d, ny)
        return q, make(lax.div(q, 2), z, core, lax.rem(q, 2))

    def zpeer(d):
        q = lax.rem(z + d, nz)
        return q, make(yhi, q, core, ylo)

    is0 = r == 0
    is1 = r == n - 1
    ishub = jnp.logical_or(is0, is1)

    def rcopy(src, dst, ssem, rsem, p):
        return pltpu.make_async_remote_copy(
            src_ref=src,
            dst_ref=dst,
            send_sem=ssem,
            recv_sem=rsem,
            device_id=dev(p),
            device_id_type=MESH,
        )

    loads = [pltpu.make_async_copy(ref, rb.at[0, i, 1], lsem.at[i]) for i, ref in enumerate((u_ref, v_ref, c_ref))]
    wloads = [pltpu.make_async_copy(ref, wraw.at[i], lsem.at[3 + i]) for i, ref in enumerate((w1_ref, t1_ref, w2_ref, t2_ref))]
    for cp in loads + wloads:
        cp.start()

    barrier = pltpu.get_barrier_semaphore()

    def greet(p):
        pl.semaphore_signal(barrier, inc=1, device_id=dev(p), device_id_type=MESH)

    @pl.when(ishub)
    def _():
        def body(i, carry):
            greet(lax.rem(r + i, n))
            return carry

        lax.fori_loop(1, n, body, 0)

    @pl.when(r != 0)
    def _():
        greet(0)

    @pl.when(r != n - 1)
    def _():
        greet(n - 1)

    for p in (up, dn, mirror, partner):
        greet(p)
    for d in range(1, ny):
        greet(ypeer(d)[1])
    for d in range(1, nz):
        greet(zpeer(d)[1])

    nbs = [[nb_ref[f, s] for s in range(4)] for f in range(6)]
    x = iota((48, 160), 0)
    yy = iota((48, 160), 1)
    xs = x & 15
    xsd = jnp.where(xs < 8, 1, 3)
    xnb = jnp.full((48, 160), -1, jnp.int32)
    for f in range(6):
        xnb = jnp.where(xs == f, nbs[f][1], xnb)
        xnb = jnp.where(xs == 8 + f, nbs[f][3], xnb)
    ym = jnp.where(yy >= 48, yy - 48, yy)
    ysd = jnp.where((ym & 15) < 8, 1, 3)
    yz = (yy - 96) & 31
    isz = yy >= 96
    yg = jnp.where(isz, yz & 7, ym & 7)
    yt = jnp.where(isz, jnp.where(yy >= 128, 2, 0), ysd)
    yfield = jnp.where(isz, yz >> 3, ym >> 4)
    way = jnp.where(isz, 1, jnp.where(yy >= 48, jnp.where(xsd == ysd, 1, 0), jnp.where(xsd == ysd, 0, 1)))
    sel[...] = onehot((xnb == 4 * yg + yt) & ((x >> 4) == yfield) & (yg < 6) & (way == 1))
    x = iota((64, 48), 0)
    yy = iota((64, 48), 1)
    xnb = jnp.full((64, 48), -1, jnp.int32)
    for f in range(6):
        xnb = jnp.where((x & 7) == f, jnp.where(x < 32, nbs[f][0], nbs[f][2]), xnb)
    yt = jnp.where((yy & 15) < 8, 1, 3)
    selh[...] = onehot((xnb == 4 * (yy & 7) + yt) & (((x & 31) >> 3) == (yy >> 4)) & ((yy & 7) < 6))

    def chosen(s, code, offset):
        t = code & 3
        flipped = (s < 2) == (t < 2)
        along = jnp.where(flipped, 1 - offset, offset - 1)
        row_tap = jnp.where(t == 0, 0, jnp.where(t == 2, 2, 1 - along))
        col_tap = jnp.where(t == 1, 2, jnp.where(t == 3, 0, 1 - along))
        return 3 * row_tap + col_tap

    xs = iota((SIDES, C), 0)
    code = jnp.full((SIDES, C), 0, jnp.int32)
    for f in range(6):
        code = jnp.where(xs == f, nbs[f][1], code)
        code = jnp.where(xs == 8 + f, nbs[f][3], code)
    side_taps = [chosen(jnp.where(xs < 8, 1, 3), code, o) for o in range(3)]

    hub_side = jnp.where(is0, 0, 2)
    hub_nb = [jnp.where(is0, nbs[f][0], nbs[f][2]) for f in range(6)]
    hub_flip = [((hub_side < 2) == ((code_f & 3) < 2)).astype(jnp.int32) for code_f in hub_nb]

    def per_face(face, values, start):
        result = jnp.full(face.shape, start, jnp.int32)
        for f in range(6):
            result = jnp.where(face == f, values[f], result)
        return result

    @pl.when(ishub)
    def _():
        a = iota((8 * F, cells), 0)
        b = iota((8 * F, cells), 1)
        g = a & 7
        pos = a >> 3
        target = g * F + jnp.where(per_face(g, hub_flip, 0) == 1, F - 1 - pos, pos)
        amat[...] = onehot((b == target) & (g < 6))

    def edges(ph, i):
        row = rb[ph, i, 1].astype(F32)
        zero = jnp.zeros((2, C), F32)
        return jnp.concatenate([row[:, F - 1], zero, row[:, 0], zero], axis=0).astype(BF)

    def prepare(ph):
        for i in range(3):
            ebuf[ph, 16 * i : 16 * i + 16] = edges(ph, i)
        hm[ph] = dot(selh[...], ebuf[ph, 0:48]).astype(BF)

        @pl.when(ishub)
        def _():
            parts = []
            for i in range(3):
                parts.append(dot(amat[...], rb[ph, i, 1].reshape(cells, C)).reshape(F, 8, C))
            parts.append(jnp.zeros((F, 8, C), F32))
            zs[ph] = jnp.concatenate(parts, axis=1).astype(BF)

        @pl.when(is0)
        def _():
            rx[ph, 0] = hm[ph, 0:32]
            ebuf[ph, 96:128] = zs[ph, 0]

        @pl.when(is1)
        def _():
            rx[ph, n - 1] = hm[ph, 32:64]
            ebuf[ph, 128:160] = zs[ph, n - 1]

    def e_copy(ph):
        return rcopy(ebuf.at[ph, pl.ds(0, 48)], ebuf.at[ph, pl.ds(48, 48)], e_s.at[ph], e_r.at[ph], mirror)

    def hm_copy(ph, h):
        return rcopy(
            hm.at[ph, pl.ds(32 * h, 32)],
            rx.at[ph, r],
            hm_s.at[ph, h],
            rx_r.at[ph, r],
            (n - 1) * h,
        )

    def z_copy(ph, h, p):
        return rcopy(zs.at[ph, p], ebuf.at[ph, pl.ds(96 + 32 * h, 32)], z_s.at[ph, p], z_r.at[ph, h], p)

    def bulk_copy(ph, i, way):
        return rcopy(
            rb.at[ph, i, 1],
            rb.at[ph, i, 2 if way == 0 else 0],
            bulk_s.at[ph, i, way],
            bulk_r.at[ph, i, way],
            up if way == 0 else dn,
        )

    def mt_copy(ph, way):
        return rcopy(
            mt.at[ph, 1],
            mt.at[ph, 2 if way == 0 else 0],
            mt_s.at[ph, way],
            mt_r.at[ph, way],
            up if way == 0 else dn,
        )

    def hub_loop(step):
        def body(i, carry):
            step(lax.rem(r + i, n))
            return carry

        lax.fori_loop(1, n, body, 0)

    def send(ph):
        for h, here in ((0, is0), (1, is1)):

            @pl.when(here)
            def _():
                hub_loop(lambda p: z_copy(ph, h, p).start())

            @pl.when(jnp.logical_not(here))
            def _():
                hm_copy(ph, h).start()

        e_copy(ph).start()
        for i in range(3):
            for way in range(2):
                bulk_copy(ph, i, way).start()

    def margins(ph):
        e_copy(ph).wait()
        for h, here in ((0, is0), (1, is1)):

            @pl.when(jnp.logical_not(here))
            def _():
                z_copy(ph, h, 0).wait_recv()

        mt[ph, 1] = dot(sel[...], ebuf[ph]).astype(BF)
        for way in range(2):
            mt_copy(ph, way).start()

    def hub_row(ph, spreads):
        @pl.when(ishub)
        def _():
            hub_loop(lambda p: rcopy(hm.at[ph, pl.ds(0, 32)], rx.at[ph, p], hm_s.at[ph, 0], rx_r.at[ph, p], p).wait_recv())
            slot = jnp.where(is0, 0, 2)
            got = rx[ph].astype(F32)
            for i in range(3):
                piece = got[:, 8 * i : 8 * i + 8].reshape(8 * F, C).astype(BF)
                row = dot(bmat[...], piece)
                row = row + dot(c0mat[...], rb[ph, i, 1].reshape(cells, C))
                row = row + dot(c2mat[...], rb[ph, i, slot].reshape(cells, C))
                row = row.astype(BF).reshape(6, F, C)
                if i in spreads:
                    mb[ph, i] = row
                    rb[ph, i, slot] = jnp.zeros((6, F, C), BF)
                else:
                    rb[ph, i, slot] = row

        @pl.when(is0)
        def _():
            mt[ph, 0] = jnp.zeros((48, C), BF)

        @pl.when(is1)
        def _():
            mt[ph, 2] = jnp.zeros((48, C), BF)

    def receive(ph, spreads):
        for way in range(2):
            for i in range(3):
                bulk_copy(ph, i, way).wait()
            mt_copy(ph, way).wait()
        hub_row(ph, spreads)

    def finish_sends(ph):
        for h, here in ((0, is0), (1, is1)):

            @pl.when(here)
            def _():
                hub_loop(lambda p: z_copy(ph, h, p).wait_send())

            @pl.when(jnp.logical_not(here))
            def _():
                hm_copy(ph, h).wait_send()

    def forward_taps(ph, i, dst):
        for a in range(3):
            padf[:, 8 : 8 + F] = rb[ph, i, a].astype(F32)
            line = mt[ph, a, 16 * i : 16 * i + 16].astype(F32)
            for f in range(6):
                padf[f, 7:8] = line[8 + f : 9 + f]
                padf[f, 8 + F : 9 + F] = line[f : f + 1]
            for b in range(3):
                k = 3 * a + b
                dst[0:cells, k * C : k * C + C] = padf[:, 7 + b : 7 + b + F].reshape(cells, C).astype(BF)

    def spread_taps(ph, i, dst, extra, scale):
        for a in range(3):
            padz[:, 8 : 8 + F] = rb[ph, i, a].astype(F32) * scale
            for b in range(3):
                k = 8 - (3 * a + b)
                dst[0:cells, k * C : k * C + C] = padz[:, 7 + b : 7 + b + F].reshape(cells, C).astype(BF)
        lines = [mt[ph, o, 16 * i : 16 * i + 16].astype(F32) * scale for o in range(3)]
        for k in range(9):
            total = jnp.zeros((SIDES, C), F32)
            for o in range(3):
                total = jnp.where(side_taps[o] == k, lines[o], total)
            dst[cells : cells + SIDES, k * C : k * C + C] = total.astype(BF)

        @pl.when(ishub)
        def _():
            padz[:, 8 : 8 + F] = mb[ph, i].astype(F32) * scale
            for f in range(6):
                picks = [chosen(hub_side, hub_nb[f], o) for o in range(3)]
                shifted = [padz[f, 7 + o : 7 + o + F] for o in range(3)]
                for k in range(9):
                    total = jnp.zeros((F, C), F32)
                    for o in range(3):
                        total = jnp.where(picks[o] == k, shifted[o], total)
                    extra[f * F : f * F + F, k * C : k * C + C] = total.astype(BF)

    def spread(dst, extra, weights, width):
        result = dot(dst[...], weights)
        field[:, :, 0:width] = result[0:cells].reshape(6, F, width)
        for f in range(6):
            field[f, F - 1 : F, 0:width] += result[cells + f : cells + f + 1]
            field[f, 0:1, 0:width] += result[cells + 8 + f : cells + 9 + f]

        @pl.when(ishub)
        def _():
            field[:, :, 0:width] += dot(extra[...], weights).reshape(6, F, width)

        return field[:, :, 0:width].reshape(cells, width)

    for cp in loads:
        cp.wait()
    prepare(0)
    base = 2 + 1 + 1 + (ny - 1) + (nz - 1)
    pl.semaphore_wait(barrier, base + 2 + jnp.where(ishub, n - 2, 0))
    send(0)

    padz[...] = jnp.zeros(padz.shape, F32)
    for cp in wloads:
        cp.wait()
    wf1[:, 0:C] = wraw[0]
    wf1[:, C : 2 * C] = wraw[1]
    for k in range(9):
        rows = slice(k * C, k * C + C)
        ws1[rows, 0:C] = wraw[0, rows].astype(F32).T.astype(BF)
        ws1[rows, C : 2 * C] = wraw[1, rows].astype(F32).T.astype(BF)
        ws2[rows, 0:C] = wraw[2, rows].astype(F32).T.astype(BF)
        ws2[rows, C : 2 * C] = wraw[3, rows].astype(F32).T.astype(BF)

    @pl.when(ishub)
    def _():
        a = iota((cells, 8 * F), 0)
        b = iota((cells, 8 * F), 1)
        face = lax.div(a, F)
        pos = a - face * F
        pos = jnp.where(per_face(face, hub_flip, 0) == 1, F - 1 - pos, pos)
        column = per_face(face, [code_f & 1 for code_f in hub_nb], 0)
        bmat[...] = onehot((b == 8 * pos + face) & (column == 1))
        a = iota((cells, cells), 0)
        b = iota((cells, cells), 1)
        face = lax.div(a, F)
        pos = a - face * F
        code_a = per_face(face, hub_nb, 0)
        other = (code_a >> 2) * F
        c0mat[...] = onehot(((code_a & 3) == hub_side) & (b == other + F - 1 - pos))
        c2mat[...] = onehot(((code_a & 3) == 2 - hub_side) & (b == other + pos))

    margins(0)
    receive(0, (2,))

    forward_taps(0, 0, tu)
    forward_taps(0, 1, tv)
    spread_taps(0, 2, ts, tx, 0.5)
    joined = dot(tu[...], wf1[...])
    hidden = joined[:, 0:C]
    hidden_tangent = joined[:, C : 2 * C] + dot(tv[...], wraw[0])
    squash = jnp.tanh(hidden)
    derivative = 1.0 - squash * squash
    act = squash.astype(BF)
    act_tangent = (derivative * hidden_tangent).astype(BF)
    aext[0:cells, 0:C] = act
    aext[0:cells, C : 2 * C] = act_tangent
    sq[...] = squash.reshape(6, F, C)
    dd[0:cells, 0:C] = (-2.0 * squash * derivative * hidden_tangent)
    back = spread(ts, tx, ws2[...], 2 * C)
    squash = sq[...].reshape(cells, C)
    derivative = 1.0 - squash * squash
    delta = (derivative * back[:, 0:C]).astype(BF)
    delta_tangent = (derivative * back[:, C : 2 * C] + dd[...] * back[:, 0:C]).astype(BF)
    rb[1, 0, 1] = aext[0:cells, 0:C].reshape(6, F, C)
    rb[1, 1, 1] = delta.reshape(6, F, C)
    rb[1, 2, 1] = delta_tangent.reshape(6, F, C)
    prepare(1)
    send(1)

    pair = jnp.concatenate([delta, delta_tangent], axis=1)
    first = dot_t(tu[...], pair)
    gsum[0, 0:K9] = first[:, 0:C]
    gsum[0, K9 : 2 * K9] = first[:, C : 2 * C] + dot_t(tv[...], delta)
    zero = jnp.zeros((2, C), F32)
    tangent = aext[0:cells, C : 2 * C].astype(F32).reshape(6, F, C)
    aext[cells : cells + SIDES, 0:C] = ebuf[1, 0:16]
    aext[cells : cells + SIDES, C : 2 * C] = jnp.concatenate(
        [tangent[:, F - 1], zero, tangent[:, 0], zero], axis=0
    ).astype(BF)
    second = dot_t(aext[...], ts[...])
    for k in range(9):
        gsum[1, k * C : k * C + C] = second[0:C, k * C : k * C + C]
        gsum[1, K9 + k * C : K9 + k * C + C] = second[C : 2 * C, k * C : k * C + C]

    @pl.when(ishub)
    def _():
        more = dot_t(aext[0:cells], tx[...])
        for k in range(9):
            gsum[1, k * C : k * C + C] += more[0:C, k * C : k * C + C]
            gsum[1, K9 + k * C : K9 + k * C + C] += more[C : 2 * C, k * C : k * C + C]

    rows_y = 2 * K9 // ny
    rows_z = rows_y // nz
    gs[...] = gsum[1 - core].astype(BF)
    core_copy = rcopy(gs, gr, c_s.at[0], c_r.at[0], partner)
    core_copy.start()
    core_copy.wait()
    total = gsum[core] + gr[...].astype(F32)
    yf[...] = total
    ys[...] = total.astype(BF)

    def y_copy(d):
        q, p = ypeer(d)
        return rcopy(ys.at[pl.ds(pl.multiple_of(q * rows_y, 16), rows_y)], yr.at[y], y_s.at[d], y_r.at[y], p)

    def y_wait(d):
        q, p = ypeer(d)
        return rcopy(ys.at[pl.ds(0, rows_y)], yr.at[q], y_s.at[d], y_r.at[q], p)

    for d in range(1, ny):
        y_copy(d).start()
    margins(1)
    for d in range(1, ny):
        y_copy(d).wait_send()
        y_wait(d).wait_recv()
    total = yf[pl.ds(pl.multiple_of(y * rows_y, 8), rows_y)]
    for d in range(1, ny):
        total = total + yr[ypeer(d)[0]].astype(F32)
    total = total.reshape(nz, rows_z, C)
    zf[...] = total
    zst[:, 0:rows_z] = total.astype(BF)
    if zst.shape[1] > rows_z:
        zst[:, rows_z:] = jnp.zeros((nz, zst.shape[1] - rows_z, C), BF)

    def z_sum_copy(d):
        q, p = zpeer(d)
        return rcopy(zst.at[q], zr.at[z], zz_s.at[d], zz_r.at[z], p)

    def z_sum_wait(d):
        q, p = zpeer(d)
        return rcopy(zst.at[q], zr.at[q], zz_s.at[d], zz_r.at[q], p)

    for d in range(1, nz):
        z_sum_copy(d).start()

    receive(1, (1, 2))
    forward_taps(1, 0, tu)
    change = dot(tu[...], wraw[2])
    next_ref[...] = (rb[0, 0, 1].astype(F32).reshape(cells, C) + 0.5 * change).astype(BF).reshape(6, F, C)
    spread_taps(1, 1, ts, tx, 1.0)
    back = spread(ts, tx, ws1[...], 2 * C)
    adj_ref[...] = (rb[0, 2, 1].astype(F32).reshape(cells, C) + back[:, 0:C]).astype(BF).reshape(6, F, C)
    dd[...] = back[:, C : 2 * C]
    spread_taps(1, 2, ty, tx, 1.0)
    back = spread(ty, tx, ws1[:, 0:C], C)
    adt_ref[...] = (dd[...] + back).astype(BF).reshape(6, F, C)

    for d in range(1, nz):
        z_sum_copy(d).wait_send()
        z_sum_wait(d).wait_recv()
    total = zf[z]
    for d in range(1, nz):
        total = total + zr[zpeer(d)[0], 0:rows_z].astype(F32)
    out_ref[core, y, z, 0:rows_z] = (total * (1.0 / F)).astype(BF)
    if zst.shape[1] > rows_z:
        out_ref[core, y, z, rows_z:] = jnp.zeros((zst.shape[1] - rows_z, C), BF)

    def gz_copy(d, q):
        return rcopy(out_ref.at[core, y, q], out_ref.at[core, y, q], gz_s.at[d], gz_r.at[q], zpeer(d)[1])

    for d in range(1, nz):
        gz_copy(d, z).start()
    for d in range(1, nz):
        gz_copy(d, z).wait_send()
        gz_copy(d, zpeer(d)[0]).wait_recv()

    def gy_copy(d, q):
        return rcopy(out_ref.at[core, q], out_ref.at[core, q], gy_s.at[d], gy_r.at[q], ypeer(d)[1])

    for d in range(1, ny):
        gy_copy(d, y).start()
    for d in range(1, ny):
        gy_copy(d, y).wait_send()
        gy_copy(d, ypeer(d)[0]).wait_recv()
    rcopy(out_ref.at[core], out_ref.at[core], gc_s.at[0], gc_r.at[0], partner).start()
    rcopy(out_ref.at[core], out_ref.at[core], gc_s.at[0], gc_r.at[0], partner).wait_send()
    rcopy(out_ref.at[1 - core], out_ref.at[1 - core], gc_s.at[0], gc_r.at[0], partner).wait_recv()
    finish_sends(0)
    finish_sends(1)


def on_device(n, ny, nz, u, v, c, w1, w2, t1, t2, nb):
    F = n
    cells = 6 * F
    rows_y = 2 * K9 // ny
    rows_z = rows_y // nz
    zp = -(-rows_z // 16) * 16
    u, v, c = (a.reshape(6, F, C) for a in (u, v, c))
    w1, w2, t1, t2 = (a.reshape(K9, C) for a in (w1, w2, t1, t2))
    vm = pltpu.VMEM
    dma = pltpu.SemaphoreType.DMA
    anywhere = pl.BlockSpec(memory_space=pl.ANY)
    inside = pl.BlockSpec(memory_space=pltpu.VMEM)
    row = jax.ShapeDtypeStruct((6, F, C), BF)
    nxt, adj, adt, out = pl.pallas_call(
        functools.partial(kernel, n, ny, nz),
        out_shape=(row, row, row, jax.ShapeDtypeStruct((2, ny, nz, zp, C), BF)),
        in_specs=[anywhere] * 7 + [pl.BlockSpec(memory_space=pltpu.SMEM)],
        out_specs=(inside,) * 4,
        scratch_shapes=[
            vm((2, 3, 3, 6, F, C), BF),
            vm((2, 3, 6, F, C), BF),
            vm((2, 160, C), BF),
            vm((2, 64, C), BF),
            vm((2, F, 32, C), BF),
            vm((2, F, 32, C), BF),
            vm((2, 3, 48, C), BF),
            vm((48, 160), BF),
            vm((64, 48), BF),
            vm((8 * F, cells), BF),
            vm((cells, 8 * F), BF),
            vm((cells, cells), BF),
            vm((cells, cells), BF),
            vm((4, K9, C), BF),
            vm((K9, 2 * C), BF),
            vm((K9, 2 * C), BF),
            vm((K9, 2 * C), BF),
            vm((6, F + 16, C), F32),
            vm((6, F + 16, C), F32),
            vm((cells, K9), BF),
            vm((cells, K9), BF),
            vm((cells + SIDES, K9), BF),
            vm((cells, K9), BF),
            vm((cells + SIDES, K9), BF),
            vm((6, F, C), F32),
            vm((cells + SIDES, 2 * C), BF),
            vm((cells, C), F32),
            vm((6, F, 2 * C), F32),
            vm((2, 2 * K9, C), F32),
            vm((2 * K9, C), BF),
            vm((2 * K9, C), BF),
            vm((2 * K9, C), F32),
            vm((2 * K9, C), BF),
            vm((ny, rows_y, C), BF),
            vm((nz, rows_z, C), F32),
            vm((nz, zp, C), BF),
            vm((nz, zp, C), BF),
            dma((7,)),
            dma((2, 3, 2)),
            dma((2, 3, 2)),
            dma((2,)),
            dma((2,)),
            dma((2, 2)),
            dma((2, n)),
            dma((2, n)),
            dma((2, 2)),
            dma((2, 2)),
            dma((2, 2)),
            dma((1,)),
            dma((1,)),
            dma((ny,)),
            dma((ny,)),
            dma((nz,)),
            dma((nz,)),
            dma((nz,)),
            dma((nz,)),
            dma((ny,)),
            dma((ny,)),
            dma((1,)),
            dma((1,)),
        ],
        compiler_params=pltpu.CompilerParams(
            collective_id=0, has_side_effects=True, vmem_limit_bytes=56 * 2**20
        ),
    )(u, v, c, w1, w2, t1, t2, nb)
    rows = out[:, :, :, :rows_z].astype(F32).reshape(2, 2, 9, C, C)
    shape = (6, 1, F, C)
    return nxt.reshape(shape), adj.reshape(shape), adt.reshape(shape), rows[:, 0], rows[:, 1]


def solution(mesh):
    n = mesh.shape["tile"] * mesh.shape["sub"]
    nz = 8 if n == 64 else 2
    ny = n // (2 * nz)
    field = P("rep", ("tile", "sub"), None, None)
    grads = P("rep", None, None, None)
    return jax.shard_map(
        functools.partial(on_device, n, ny, nz),
        mesh=mesh,
        in_specs=(field, field, field, P(), P(), P(), P(), P()),
        out_specs=(field, field, field, grads, grads),
        check_vma=False,
    )
```

time: 1040 us -> 84.5 us (0.08)
  blocking collectives: 500 us -> 0 us
  waiting for transfers between devices: 369 us -> 0 us
  Pallas kernels: 0 us -> 76.9 us
  local copies, waits for them, and re-layouts: 54.9 us -> 6.21 us
  matrix products: 47.7 us -> 0 us
  starting transfers between devices: 27.8 us -> 0 us
  other arithmetic: 18.1 us -> 0.26 us
  between operations: 16 us -> 0.68 us
    all_gather x4 -> x0, blocking collectives: 500 us -> none  [face_halo(): columns = lax.all_gather(side_rims, ('tile', 'sub'), axis=3, tiled=True)]
    psum x3 -> x0, waiting for transfers between devices: 360 us -> none  [the longest x1 183 us: on_device(): lax.psum((grad_first, grad_second, curve_first, curve_second), ('tile', '...]
    pallas_call x0 -> x1, Pallas kernels: none -> 76.9 us  [on_device(): pl.pallas_call(functools.partial(kernel, n, ny, nz), out_shape=(row, row,...]
    dot_general x79 -> x0, matrix products: 47.7 us -> none  [the longest x60 31.8 us: along_line(): jnp.einsum('flo,fio->fli', margin_line[:, offset:offset + length], kernel...]
    ppermute x8 -> x0, starting transfers between devices: 27.5 us -> none  [the longest x4 16.8 us: extended(): lax.ppermute(head, axis, [((i + 1) % count, i) for i in range(ends)])]
    slice x18 -> x1, local copies, waits for them, and re-layouts: 27.2 us -> 1.37 us  [on_device(): rows = out[:, :, :, :rows_z].astype(F32).reshape(2, 2, 9, C, C)]
  transfers between devices with their start and end apart: 11 -> 0, of which waited for: 3 -> 0; matrix products, arithmetic and copies ran while one was open for 7% -> 0% of each run, Pallas kernels for 0% -> 0%
where the time goes in v1:
time: 84.5 us; the launch traced here: 84.1 us
  Pallas kernels  76.9 us (91%)
  local copies, waits for them, and re-layouts  6.21 us (7%)
    pallas_call x1, Pallas kernels, on_device(): pl.pallas_call(functools.partial(kernel, n, ny, nz), out_shape=(row, row,...  76.9 us
    unnamed x10, local copies, waits for them, and re-layouts  3.29 us

profile of v1, /device:TPU:1, one launch (start us, length us, event | category | flops | bytes accessed | tf_op | source)
XLA Modules:
  0.0 84.1 jit_solution(15235486956056520885)
XLA Ops:
  0.6 1.4 %copy.13.nb_ref = s32[6,4]{1,0:T(8,128)} copy(s32[6,4]{0,1:T(4,128)} %param.15) | data formatting | bytes 192 | tf_op args[7]
  2.0 76.9 %shard_map.119 = (bf16[6,64,128]{2,1,0:T(8,128)(2,1)}, bf16[6,64,128]{2,1,0:T(8,128)(2,1)}, bf16[6,64,128]{2,1,0:T(8,128)(2,1)}, bf16[2,4,8,80,128]{4,3,2,1,0:T(8,128)(2,1)}) custom-call(bf16[6,64,128]{2,1,0:T(8,128)(2,1)} %bitcast.31, bf16[6,64,128]{2,1,0:T(8,128)(2,1)} %bitcast.32, bf16[6,64,128]{2,1,0:T(8,128)(2,1)} %bitcast.33, ...), custom_call_target="tpu_custom_call" | custom-call | tf_op jit(solution)/shard_map/pallas_call | solution.py:626
  78.9 1.4 %slice.9 = bf16[2,4,8,72,128]{4,3,2,1,0:T(8,128)(2,1)S(1)} slice(bf16[2,4,8,80,128]{4,3,2,1,0:T(8,128)(2,1)} %get-tuple-element.12), slice={[0:2], [0:4], [0:8], [0:72], [0:128]} | slice | bytes 2359296 | tf_op jit(solution)/shard_map/slice | solution.py:697
  80.3 0.3 convert.1
  80.6 0.0 copy-start.2
  80.6 0.0 copy-start.1
  80.6 0.0 copy-start
  80.6 1.6 %slice_bitcast_fusion = (f32[2,9,128,128]{3,2,1,0:T(8,128)}, f32[2,9,128,128]{3,2,1,0:T(8,128)}) fusion(f32[2,2,9,128,128]{4,3,2,1,0:T(8,128)S(1)} %convert.1), kind=kLoop, calls=%fused_computation | loop fusion | bytes 4718592 | tf_op jit(solution)/shard_map/squeeze | solution.py:699
  82.1 0.0 copy-done.2
  82.1 0.6 copy.24
  82.8 0.0 copy-done.1
  82.8 0.6 copy.25
  83.4 0.0 copy-done
  83.4 0.6 copy.26
Async XLA Ops:
  80.6 1.6 %copy-start.2 = (bf16[6,64,128]{2,1,0:T(8,128)(2,1)S(1)}, bf16[6,64,128]{2,1,0:T(8,128)(2,1)}, u32[]{:S(2)}) copy-start(bf16[6,64,128]{2,1,0:T(8,128)(2,1)} %get-tuple-element.9) | copy-start | bytes 294916
  80.6 2.2 %copy-start.1 = (bf16[6,64,128]{2,1,0:T(8,128)(2,1)S(1)}, bf16[6,64,128]{2,1,0:T(8,128)(2,1)}, u32[]{:S(2)}) copy-start(bf16[6,64,128]{2,1,0:T(8,128)(2,1)} %get-tuple-element.10) | copy-start | bytes 294916
  80.6 2.9 %copy-start = (bf16[6,64,128]{2,1,0:T(8,128)(2,1)S(1)}, bf16[6,64,128]{2,1,0:T(8,128)(2,1)}, u32[]{:S(2)}) copy-start(bf16[6,64,128]{2,1,0:T(8,128)(2,1)} %get-tuple-element.11) | copy-start | bytes 294916

commit v2 on v1

--- a/solution.py
+++ b/solution.py
@@ -78,12 +78,19 @@
     gsum,
     gs,
     gr,
-    yf,
-    ys,
-    yr,
-    zf,
-    zst,
-    zr,
+    pf,
+    ps,
+    pr,
+    qf,
+    qs,
+    qr,
+    pz,
+    pzf,
+    pzr,
+    qy,
+    qyf,
+    qyr,
+    nbm,
     lsem,
     bulk_s,
     bulk_r,
@@ -95,18 +102,8 @@
     z_r,
     mt_s,
     mt_r,
-    c_s,
-    c_r,
-    y_s,
-    y_r,
-    zz_s,
-    zz_r,
-    gz_s,
-    gz_r,
-    gy_s,
-    gy_r,
-    gc_s,
-    gc_r,
+    ar_s,
+    ar_r,
 ):
     F = n
     cells = 6 * F
@@ -151,6 +148,8 @@
             device_id_type=MESH,
         )
 
+    nbload = pltpu.make_async_copy(nb_ref, nbm, lsem.at[7])
+    nbload.start()
     loads = [pltpu.make_async_copy(ref, rb.at[0, i, 1], lsem.at[i]) for i, ref in enumerate((u_ref, v_ref, c_ref))]
     wloads = [pltpu.make_async_copy(ref, wraw.at[i], lsem.at[3 + i]) for i, ref in enumerate((w1_ref, t1_ref, w2_ref, t2_ref))]
     for cp in loads + wloads:
@@ -184,7 +183,8 @@
     for d in range(1, nz):
         greet(zpeer(d)[1])
 
-    nbs = [[nb_ref[f, s] for s in range(4)] for f in range(6)]
+    nbload.wait()
+    nbs = [[nbm[f, s] for s in range(4)] for f in range(6)]
     x = iota((48, 160), 0)
     yy = iota((48, 160), 1)
     xs = x & 15
@@ -500,8 +500,8 @@
 
     pair = jnp.concatenate([delta, delta_tangent], axis=1)
     first = dot_t(tu[...], pair)
-    gsum[0, 0:K9] = first[:, 0:C]
-    gsum[0, K9 : 2 * K9] = first[:, C : 2 * C] + dot_t(tv[...], delta)
+    gsum[0:K9] = first[:, 0:C]
+    gsum[2 * K9 : 3 * K9] = first[:, C : 2 * C] + dot_t(tv[...], delta)
     zero = jnp.zeros((2, C), F32)
     tangent = aext[0:cells, C : 2 * C].astype(F32).reshape(6, F, C)
     aext[cells : cells + SIDES, 0:C] = ebuf[1, 0:16]
@@ -510,112 +510,260 @@
     ).astype(BF)
     second = dot_t(aext[...], ts[...])
     for k in range(9):
-        gsum[1, k * C : k * C + C] = second[0:C, k * C : k * C + C]
-        gsum[1, K9 + k * C : K9 + k * C + C] = second[C : 2 * C, k * C : k * C + C]
+        gsum[K9 + k * C : K9 + k * C + C] = second[0:C, k * C : k * C + C]
+        gsum[3 * K9 + k * C : 3 * K9 + k * C + C] = second[C : 2 * C, k * C : k * C + C]
 
     @pl.when(ishub)
     def _():
         more = dot_t(aext[0:cells], tx[...])
         for k in range(9):
-            gsum[1, k * C : k * C + C] += more[0:C, k * C : k * C + C]
-            gsum[1, K9 + k * C : K9 + k * C + C] += more[C : 2 * C, k * C : k * C + C]
-
-    rows_y = 2 * K9 // ny
-    rows_z = rows_y // nz
-    gs[...] = gsum[1 - core].astype(BF)
-    core_copy = rcopy(gs, gr, c_s.at[0], c_r.at[0], partner)
-    core_copy.start()
-    core_copy.wait()
-    total = gsum[core] + gr[...].astype(F32)
-    yf[...] = total
-    ys[...] = total.astype(BF)
-
-    def y_copy(d):
-        q, p = ypeer(d)
-        return rcopy(ys.at[pl.ds(pl.multiple_of(q * rows_y, 16), rows_y)], yr.at[y], y_s.at[d], y_r.at[y], p)
-
-    def y_wait(d):
-        q, p = ypeer(d)
-        return rcopy(ys.at[pl.ds(0, rows_y)], yr.at[q], y_s.at[d], y_r.at[q], p)
-
-    for d in range(1, ny):
-        y_copy(d).start()
+            gsum[K9 + k * C : K9 + k * C + C] += more[0:C, k * C : k * C + C]
+            gsum[3 * K9 + k * C : 3 * K9 + k * C + C] += more[C : 2 * C, k * C : k * C + C]
+
+    shard, p0, p1, qn = split_rows(ny, nz)
+    qoff = p0 + p1 + qn * core
+    qother = p0 + p1 + qn * (1 - core)
+    slots = {}
+    for name, count in PHASES:
+        slots[name] = sum(ny if c == "y" else nz if c == "z" else 1 for _, c in PHASES[: len(slots)])
+
+    def by_core(fn):
+        @pl.when(core == 0)
+        def _():
+            fn(0, p0, p0, p1)
+
+        @pl.when(core == 1)
+        def _():
+            fn(p0, p1, 0, p0)
+
+    def ar(name, slot_s, slot_r, src, dst, p):
+        return rcopy(src, dst, ar_s.at[slots[name] + slot_s], ar_r.at[slots[name] + slot_r], p)
+
+    ypeers = [ypeer(d) for d in range(1, ny)]
+    zpeers = [zpeer(d) for d in range(1, nz)]
+    whole = gsum[...].reshape(ny, nz, shard, C)
+    gs[...] = whole.astype(BF)
+
+    def core_p(off, size, ooff, osize):
+        return ar("cp", 0, 0, gs.at[:, :, pl.ds(ooff, osize)], gr.at[:, :, pl.ds(ooff, osize)], partner)
+
+    def core_p_in(off, size, ooff, osize):
+        return ar("cp", 0, 0, gs.at[:, :, pl.ds(off, size)], gr.at[:, :, pl.ds(off, size)], partner)
+
+    def core_q(o):
+        return ar("cq", 0, 0, gs.at[:, :, pl.ds(o, qn)], gr.at[:, :, pl.ds(o, qn)], partner)
+
+    core_q(qother).start()
+    by_core(lambda *a: core_p(*a).start())
+
+    def q1(d, out):
+        q, p = zpeers[d]
+        return ar("q1", q, z if out else q, qs.at[:, q], qr.at[z if out else q], p)
+
+    def p1_copy(d, size, out):
+        q, p = ypeers[d]
+        return ar("p1", q, y if out else q, ps.at[q, :, pl.ds(0, size)], pr.at[y if out else q, :, pl.ds(0, size)], p)
+
+    core_q(qother).wait_send()
+    core_q(qoff).wait_recv()
+
+    def stage(qo):
+        part = gsum[...].reshape(ny, nz, shard, C)[:, :, qo : qo + qn] + gr[:, :, qo : qo + qn].astype(F32)
+        qf[...] = part
+        qs[...] = part.astype(BF)
+
+    by_core(lambda off, size, ooff, osize: stage(p0 + p1 if off == 0 else p0 + p1 + qn))
+    for d in range(nz - 1):
+        q1(d, True).start()
+
+    def stage(off, size, ooff, osize):
+        core_p(off, size, ooff, osize).wait_send()
+        core_p_in(off, size, ooff, osize).wait_recv()
+        part = gsum[...].reshape(ny, nz, shard, C)[:, :, off : off + size] + gr[:, :, off : off + size].astype(F32)
+        pf[:, :, 0:size] = part
+        ps[:, :, 0:size] = part.astype(BF)
+        for d in range(ny - 1):
+            p1_copy(d, size, True).start()
+
+    by_core(stage)
     margins(1)
-    for d in range(1, ny):
-        y_copy(d).wait_send()
-        y_wait(d).wait_recv()
-    total = yf[pl.ds(pl.multiple_of(y * rows_y, 8), rows_y)]
-    for d in range(1, ny):
-        total = total + yr[ypeer(d)[0]].astype(F32)
-    total = total.reshape(nz, rows_z, C)
-    zf[...] = total
-    zst[:, 0:rows_z] = total.astype(BF)
-    if zst.shape[1] > rows_z:
-        zst[:, rows_z:] = jnp.zeros((nz, zst.shape[1] - rows_z, C), BF)
-
-    def z_sum_copy(d):
-        q, p = zpeer(d)
-        return rcopy(zst.at[q], zr.at[z], zz_s.at[d], zz_r.at[z], p)
-
-    def z_sum_wait(d):
-        q, p = zpeer(d)
-        return rcopy(zst.at[q], zr.at[q], zz_s.at[d], zz_r.at[q], p)
-
-    for d in range(1, nz):
-        z_sum_copy(d).start()
+
+    def p2_copy(d, size, out):
+        q, p = zpeers[d]
+        return ar("p2", q, z if out else q, pz.at[q, pl.ds(0, size)], pzr.at[z if out else q, pl.ds(0, size)], p)
+
+    def stage(off, size, ooff, osize):
+        for d in range(ny - 1):
+            p1_copy(d, size, True).wait_send()
+            p1_copy(d, size, False).wait_recv()
+        part = pf[y, :, 0:size]
+        for q, p in ypeers:
+            part = part + pr[q, :, 0:size].astype(F32)
+        pzf[:, 0:size] = part
+        pz[:, 0:size] = part.astype(BF)
+        for d in range(nz - 1):
+            p2_copy(d, size, True).start()
+
+    by_core(stage)
+
+    def q2(d, out):
+        q, p = ypeers[d]
+        return ar("q2", q, y if out else q, qy.at[q], qyr.at[y if out else q], p)
+
+    for d in range(nz - 1):
+        q1(d, True).wait_send()
+        q1(d, False).wait_recv()
+    part = qf[:, z]
+    for q, p in zpeers:
+        part = part + qr[q].astype(F32)
+    qyf[...] = part
+    qy[...] = part.astype(BF)
+    for d in range(ny - 1):
+        q2(d, True).start()
 
     receive(1, (1, 2))
     forward_taps(1, 0, tu)
     change = dot(tu[...], wraw[2])
     next_ref[...] = (rb[0, 0, 1].astype(F32).reshape(cells, C) + 0.5 * change).astype(BF).reshape(6, F, C)
+
+    scale = 1.0 / F
+
+    def p3(d, size, off, out):
+        q, p = zpeers[d]
+        zz = z if out else q
+        ref = out_ref.at[y, zz, pl.ds(off, size)]
+        return ar("p3", q, zz, ref, ref, p)
+
+    def stage(off, size, ooff, osize):
+        for d in range(nz - 1):
+            p2_copy(d, size, True).wait_send()
+            p2_copy(d, size, False).wait_recv()
+        part = pzf[z, 0:size]
+        for q, p in zpeers:
+            part = part + pzr[q, 0:size].astype(F32)
+        out_ref[y, z, off : off + size] = (part * scale).astype(BF)
+        for d in range(nz - 1):
+            p3(d, size, off, True).start()
+
+    by_core(stage)
+
+    def q3(d, out):
+        q, p = ypeers[d]
+        qq = y if out else q
+        ref = out_ref.at[qq, z, pl.ds(qoff, qn)]
+        return ar("q3", q, qq, ref, ref, p)
+
+    for d in range(ny - 1):
+        q2(d, True).wait_send()
+        q2(d, False).wait_recv()
+    part = qyf[y]
+    for q, p in ypeers:
+        part = part + qyr[q].astype(F32)
+    out_ref[y, z, pl.ds(pl.multiple_of(qoff, 16), qn)] = (part * scale).astype(BF)
+    for d in range(ny - 1):
+        q3(d, True).start()
+
     spread_taps(1, 1, ts, tx, 1.0)
     back = spread(ts, tx, ws1[...], 2 * C)
     adj_ref[...] = (rb[0, 2, 1].astype(F32).reshape(cells, C) + back[:, 0:C]).astype(BF).reshape(6, F, C)
     dd[...] = back[:, C : 2 * C]
+
+    def p4(d, size, off, out):
+        q, p = ypeers[d]
+        qq = y if out else q
+        ref = out_ref.at[qq, :, pl.ds(off, size)]
+        return ar("p4", q, qq, ref, ref, p)
+
+    def cpy_p(q, size, off):
+        ref = out_ref.at[q, :, pl.ds(off, size)]
+        return ar("c4", q, q, ref, ref, partner)
+
+    def stage(off, size, ooff, osize):
+        for d in range(nz - 1):
+            p3(d, size, off, True).wait_send()
+            p3(d, size, off, False).wait_recv()
+        for d in range(ny - 1):
+            p4(d, size, off, True).start()
+        cpy_p(y, size, off).start()
+
+    by_core(stage)
+
+    def q4(d, out):
+        q, p = zpeers[d]
+        qq = z if out else q
+        ref = out_ref.at[:, qq, pl.ds(qoff, qn)]
+        return ar("q4", q, qq, ref, ref, p)
+
+    def cpy_q(q, o):
+        ref = out_ref.at[:, q, pl.ds(o, qn)]
+        return ar("d4", q, q, ref, ref, partner)
+
+    for d in range(ny - 1):
+        q3(d, True).wait_send()
+        q3(d, False).wait_recv()
+    for d in range(nz - 1):
+        q4(d, True).start()
+    cpy_q(z, qoff).start()
+
     spread_taps(1, 2, ty, tx, 1.0)
     back = spread(ty, tx, ws1[:, 0:C], C)
     adt_ref[...] = (dd[...] + back).astype(BF).reshape(6, F, C)
 
-    for d in range(1, nz):
-        z_sum_copy(d).wait_send()
-        z_sum_wait(d).wait_recv()
-    total = zf[z]
-    for d in range(1, nz):
-        total = total + zr[zpeer(d)[0], 0:rows_z].astype(F32)
-    out_ref[core, y, z, 0:rows_z] = (total * (1.0 / F)).astype(BF)
-    if zst.shape[1] > rows_z:
-        out_ref[core, y, z, rows_z:] = jnp.zeros((zst.shape[1] - rows_z, C), BF)
-
-    def gz_copy(d, q):
-        return rcopy(out_ref.at[core, y, q], out_ref.at[core, y, q], gz_s.at[d], gz_r.at[q], zpeer(d)[1])
-
-    for d in range(1, nz):
-        gz_copy(d, z).start()
-    for d in range(1, nz):
-        gz_copy(d, z).wait_send()
-        gz_copy(d, zpeer(d)[0]).wait_recv()
-
-    def gy_copy(d, q):
-        return rcopy(out_ref.at[core, q], out_ref.at[core, q], gy_s.at[d], gy_r.at[q], ypeer(d)[1])
-
-    for d in range(1, ny):
-        gy_copy(d, y).start()
-    for d in range(1, ny):
-        gy_copy(d, y).wait_send()
-        gy_copy(d, ypeer(d)[0]).wait_recv()
-    rcopy(out_ref.at[core], out_ref.at[core], gc_s.at[0], gc_r.at[0], partner).start()
-    rcopy(out_ref.at[core], out_ref.at[core], gc_s.at[0], gc_r.at[0], partner).wait_send()
-    rcopy(out_ref.at[1 - core], out_ref.at[1 - core], gc_s.at[0], gc_r.at[0], partner).wait_recv()
+    def stage(off, size, ooff, osize):
+        for d in range(ny - 1):
+            p4(d, size, off, False).wait_recv()
+            cpy_p(ypeers[d][0], size, off).start()
+
+    by_core(stage)
+    for d in range(nz - 1):
+        q4(d, False).wait_recv()
+        cpy_q(zpeers[d][0], qoff).start()
+
+    def stage(off, size, ooff, osize):
+        for d in range(ny - 1):
+            p4(d, size, off, True).wait_send()
+        for q in range(ny):
+            cpy_p(q, size, off).wait_send()
+            cpy_p(q, osize, ooff).wait_recv()
+
+    by_core(stage)
+    for d in range(nz - 1):
+        q4(d, True).wait_send()
+    for q in range(nz):
+        cpy_q(q, qoff).wait_send()
+        cpy_q(q, qother).wait_recv()
     finish_sends(0)
     finish_sends(1)
+
+
+PHASES = (
+    ("cp", "1"),
+    ("cq", "1"),
+    ("q1", "z"),
+    ("p1", "y"),
+    ("p2", "z"),
+    ("q2", "y"),
+    ("p3", "z"),
+    ("q3", "y"),
+    ("p4", "y"),
+    ("c4", "y"),
+    ("q4", "z"),
+    ("d4", "z"),
+)
+
+
+def split_rows(ny, nz):
+    tiles = 4 * K9 // (16 * ny * nz)
+    qn = 2 * tiles // 9
+    p1 = (tiles - 2 * qn) // 2
+    return 16 * tiles, 16 * (tiles - 2 * qn - p1), 16 * p1, 16 * qn
 
 
 def on_device(n, ny, nz, u, v, c, w1, w2, t1, t2, nb):
     F = n
     cells = 6 * F
-    rows_y = 2 * K9 // ny
-    rows_z = rows_y // nz
-    zp = -(-rows_z // 16) * 16
+    shard, p0, p1, qn = split_rows(ny, nz)
+    arrived = sum(ny if c == "y" else nz if c == "z" else 1 for _, c in PHASES)
     u, v, c = (a.reshape(6, F, C) for a in (u, v, c))
     w1, w2, t1, t2 = (a.reshape(K9, C) for a in (w1, w2, t1, t2))
     vm = pltpu.VMEM
@@ -625,8 +773,8 @@
     row = jax.ShapeDtypeStruct((6, F, C), BF)
     nxt, adj, adt, out = pl.pallas_call(
         functools.partial(kernel, n, ny, nz),
-        out_shape=(row, row, row, jax.ShapeDtypeStruct((2, ny, nz, zp, C), BF)),
-        in_specs=[anywhere] * 7 + [pl.BlockSpec(memory_space=pltpu.SMEM)],
+        out_shape=(row, row, row, jax.ShapeDtypeStruct((ny, nz, shard, C), BF)),
+        in_specs=[anywhere] * 8,
         out_specs=(inside,) * 4,
         scratch_shapes=[
             vm((2, 3, 3, 6, F, C), BF),
@@ -657,16 +805,23 @@
             vm((cells + SIDES, 2 * C), BF),
             vm((cells, C), F32),
             vm((6, F, 2 * C), F32),
-            vm((2, 2 * K9, C), F32),
-            vm((2 * K9, C), BF),
-            vm((2 * K9, C), BF),
-            vm((2 * K9, C), F32),
-            vm((2 * K9, C), BF),
-            vm((ny, rows_y, C), BF),
-            vm((nz, rows_z, C), F32),
-            vm((nz, zp, C), BF),
-            vm((nz, zp, C), BF),
-            dma((7,)),
+            vm((4 * K9, C), F32),
+            vm((ny, nz, shard, C), BF),
+            vm((ny, nz, shard, C), BF),
+            vm((ny, nz, p0, C), F32),
+            vm((ny, nz, p0, C), BF),
+            vm((ny, nz, p0, C), BF),
+            vm((ny, nz, qn, C), F32),
+            vm((ny, nz, qn, C), BF),
+            vm((nz, ny, qn, C), BF),
+            vm((nz, p0, C), BF),
+            vm((nz, p0, C), F32),
+            vm((nz, p0, C), BF),
+            vm((ny, qn, C), BF),
+            vm((ny, qn, C), F32),
+            vm((ny, qn, C), BF),
+            pltpu.SMEM((6, 4), jnp.int32),
+            dma((8,)),
             dma((2, 3, 2)),
             dma((2, 3, 2)),
             dma((2,)),
@@ -677,26 +832,16 @@
             dma((2, 2)),
             dma((2, 2)),
             dma((2, 2)),
-            dma((1,)),
-            dma((1,)),
-            dma((ny,)),
-            dma((ny,)),
-            dma((nz,)),
-            dma((nz,)),
-            dma((nz,)),
-            dma((nz,)),
-            dma((ny,)),
-            dma((ny,)),
-            dma((1,)),
-            dma((1,)),
+            dma((arrived,)),
+            dma((arrived,)),
         ],
         compiler_params=pltpu.CompilerParams(
             collective_id=0, has_side_effects=True, vmem_limit_bytes=56 * 2**20
         ),
     )(u, v, c, w1, w2, t1, t2, nb)
-    rows = out[:, :, :, :rows_z].astype(F32).reshape(2, 2, 9, C, C)
+    grads = out.reshape(2, 2, 9, C, C).astype(F32)
     shape = (6, 1, F, C)
-    return nxt.reshape(shape), adj.reshape(shape), adt.reshape(shape), rows[:, 0], rows[:, 1]
+    return nxt.reshape(shape), adj.reshape(shape), adt.reshape(shape), grads[0], grads[1]
 
 
 def solution(mesh):

time: 84.5 us -> 76.7 us (0.908)
  Pallas kernels: 76.9 us -> 69.4 us
    pallas_call x1, Pallas kernels: 76.9 us -> 69.4 us  [on_device(): pl.pallas_call(functools.partial(kernel, n, ny, nz), out_shape=(row, row,...]
    squeeze x1 -> x0, local copies, waits for them, and re-layouts: 1.55 us -> none  [on_device(): rows[:, 1]]
    slice x1, local copies, waits for them, and re-layouts: 1.37 us -> 2.89 us  [on_device(): grads[1]]
where the time goes in v2:
time: 76.7 us; the launch traced here: 76.3 us
  Pallas kernels  69.4 us (90%)
  local copies, waits for them, and re-layouts  6.17 us (8%)
    pallas_call x1, Pallas kernels, on_device(): pl.pallas_call(functools.partial(kernel, n, ny, nz), out_shape=(row, row,...  69.4 us
    unnamed x10, local copies, waits for them, and re-layouts  3.29 us
    slice x1, local copies, waits for them, and re-layouts, on_device(): grads[1]  2.89 us

profile of v2, /device:TPU:1, one launch (start us, length us, event | category | flops | bytes accessed | tf_op | source)
XLA Modules:
  0.0 76.3 jit_solution(18147582437985326520)
XLA Ops:
  0.6 1.4 %copy.13.nb_ref = s32[6,4]{1,0:T(8,128)} copy(s32[6,4]{0,1:T(4,128)} %param.15) | data formatting | bytes 192 | tf_op args[7]
  2.0 69.4 %shard_map.119 = (bf16[6,64,128]{2,1,0:T(8,128)(2,1)}, bf16[6,64,128]{2,1,0:T(8,128)(2,1)}, bf16[6,64,128]{2,1,0:T(8,128)(2,1)}, bf16[4,8,144,128]{3,2,1,0:T(8,128)(2,1)}) custom-call(bf16[6,64,128]{2,1,0:T(8,128)(2,1)} %bitcast.24, bf16[6,64,128]{2,1,0:T(8,128)(2,1)} %bitcast.25, bf16[6,64,128]{2,1,0:T(8,128)(2,1)} %bitcast.26, bf16[1152,128]{1,0:T(8,128)(2,1)} %bitcast.20, ...), custom_call_target="tpu_custom_call" | custom-call | tf_op jit(solution)/shard_map/pallas_call | solution.py:774
  71.4 0.0 copy-start.2
  71.4 0.0 copy-start.1
  71.5 0.0 copy-start
  71.5 2.9 %fusion = (f32[2,8,144,128]{3,2,1,0:T(8,128)}, f32[2,8,144,128]{3,2,1,0:T(8,128)}) fusion(bf16[4,8,144,128]{3,2,1,0:T(8,128)(2,1)} %get-tuple-element.12), kind=kLoop, calls=%fused_computation | loop fusion | bytes 4718592 | tf_op jit(solution)/shard_map/slice | solution.py:844
  74.3 0.0 copy-done.2
  74.4 0.6 copy.20
  75.0 0.0 copy-done.1
  75.0 0.6 copy.21
  75.6 0.0 copy-done
  75.6 0.6 copy.22
Async XLA Ops:
  71.4 2.9 %copy-start.2 = (bf16[6,64,128]{2,1,0:T(8,128)(2,1)S(1)}, bf16[6,64,128]{2,1,0:T(8,128)(2,1)}, u32[]{:S(2)}) copy-start(bf16[6,64,128]{2,1,0:T(8,128)(2,1)} %get-tuple-element.9) | copy-start | bytes 294916
  71.4 3.6 %copy-start.1 = (bf16[6,64,128]{2,1,0:T(8,128)(2,1)S(1)}, bf16[6,64,128]{2,1,0:T(8,128)(2,1)}, u32[]{:S(2)}) copy-start(bf16[6,64,128]{2,1,0:T(8,128)(2,1)} %get-tuple-element.10) | copy-start | bytes 294916
  71.5 4.2 %copy-start = (bf16[6,64,128]{2,1,0:T(8,128)(2,1)S(1)}, bf16[6,64,128]{2,1,0:T(8,128)(2,1)}, u32[]{:S(2)}) copy-start(bf16[6,64,128]{2,1,0:T(8,128)(2,1)} %get-tuple-element.11) | copy-start | bytes 294916

commit v3 on v2

--- a/solution.py
+++ b/solution.py
@@ -64,16 +64,14 @@
     wf1,
     ws1,
     ws2,
-    padf,
     padz,
     tu,
     tv,
     ts,
     tx,
-    ty,
-    sq,
     aext,
-    dd,
+    pext,
+    front,
     field,
     gsum,
     gs,
@@ -91,6 +89,10 @@
     qyf,
     qyr,
     nbm,
+    res,
+    fin_p,
+    fin_q,
+    osem,
     lsem,
     bulk_s,
     bulk_r,
@@ -184,7 +186,7 @@
         greet(zpeer(d)[1])
 
     nbload.wait()
-    nbs = [[nbm[f, s] for s in range(4)] for f in range(6)]
+    nbs = [[nbm[s, f] for s in range(4)] for f in range(6)]
     x = iota((48, 160), 0)
     yy = iota((48, 160), 1)
     xs = x & 15
@@ -296,6 +298,11 @@
             up if way == 0 else dn,
         )
 
+    def send_rows(ph):
+        for i in range(3):
+            for way in range(2):
+                bulk_copy(ph, i, way).start()
+
     def mt_copy(ph, way):
         return rcopy(
             mt.at[ph, 1],
@@ -324,9 +331,6 @@
                 hm_copy(ph, h).start()
 
         e_copy(ph).start()
-        for i in range(3):
-            for way in range(2):
-                bulk_copy(ph, i, way).start()
 
     def margins(ph):
         e_copy(ph).wait()
@@ -358,6 +362,16 @@
                 else:
                     rb[ph, i, slot] = row
 
+    def receive(ph, spreads):
+        for i in range(3):
+            for way in range(2):
+                bulk_copy(ph, i, way).wait()
+        hub_row(ph, spreads)
+
+    def receive_margins(ph):
+        for way in range(2):
+            mt_copy(ph, way).wait()
+
         @pl.when(is0)
         def _():
             mt[ph, 0] = jnp.zeros((48, C), BF)
@@ -366,13 +380,6 @@
         def _():
             mt[ph, 2] = jnp.zeros((48, C), BF)
 
-    def receive(ph, spreads):
-        for way in range(2):
-            for i in range(3):
-                bulk_copy(ph, i, way).wait()
-            mt_copy(ph, way).wait()
-        hub_row(ph, spreads)
-
     def finish_sends(ph):
         for h, here in ((0, is0), (1, is1)):
 
@@ -384,23 +391,22 @@
             def _():
                 hm_copy(ph, h).wait_send()
 
-    def forward_taps(ph, i, dst):
+    def row_taps(ph, i, a, dst, spreads, scale):
+        padz[:, 8 : 8 + F] = rb[ph, i, a].astype(F32) * scale
+        for b in range(3):
+            k = 3 * a + b
+            k = 8 - k if spreads else k
+            dst[0:cells, k * C : k * C + C] = padz[:, 7 + b : 7 + b + F].reshape(cells, C).astype(BF)
+
+    def forward_sides(ph, i, dst):
         for a in range(3):
-            padf[:, 8 : 8 + F] = rb[ph, i, a].astype(F32)
             line = mt[ph, a, 16 * i : 16 * i + 16].astype(F32)
-            for f in range(6):
-                padf[f, 7:8] = line[8 + f : 9 + f]
-                padf[f, 8 + F : 9 + F] = line[f : f + 1]
-            for b in range(3):
+            zero = jnp.zeros((SIDES, C), F32)
+            for b, part in enumerate((jnp.where(xs < 8, zero, line), zero, jnp.where(xs < 8, line, zero))):
                 k = 3 * a + b
-                dst[0:cells, k * C : k * C + C] = padf[:, 7 + b : 7 + b + F].reshape(cells, C).astype(BF)
-
-    def spread_taps(ph, i, dst, extra, scale):
-        for a in range(3):
-            padz[:, 8 : 8 + F] = rb[ph, i, a].astype(F32) * scale
-            for b in range(3):
-                k = 8 - (3 * a + b)
-                dst[0:cells, k * C : k * C + C] = padz[:, 7 + b : 7 + b + F].reshape(cells, C).astype(BF)
+                dst[cells : cells + SIDES, k * C : k * C + C] = part.astype(BF)
+
+    def spread_sides(ph, i, dst, scale):
         lines = [mt[ph, o, 16 * i : 16 * i + 16].astype(F32) * scale for o in range(3)]
         for k in range(9):
             total = jnp.zeros((SIDES, C), F32)
@@ -408,37 +414,38 @@
                 total = jnp.where(side_taps[o] == k, lines[o], total)
             dst[cells : cells + SIDES, k * C : k * C + C] = total.astype(BF)
 
+    def hub_taps(ph, i, extra, scale):
+        padz[:, 8 : 8 + F] = mb[ph, i].astype(F32) * scale
+        for f in range(6):
+            picks = [chosen(hub_side, hub_nb[f], o) for o in range(3)]
+            shifted = [padz[f, 7 + o : 7 + o + F] for o in range(3)]
+            for k in range(9):
+                total = jnp.zeros((F, C), F32)
+                for o in range(3):
+                    total = jnp.where(picks[o] == k, shifted[o], total)
+                extra[f * F : f * F + F, k * C : k * C + C] = total.astype(BF)
+
+    def add_sides(ref, lanes, side):
+        for f in range(6):
+            ref[f, F - 1 : F, lanes] += side[f : f + 1]
+            ref[f, 0:1, lanes] += side[8 + f : 9 + f]
+
+    def main_spread(ph, i, dst, extra, weights, scale, ref, lanes):
+        width = lanes.stop - lanes.start
+        ref[:, :, lanes] = dot(dst[0:cells], weights).reshape(6, F, width)
+
         @pl.when(ishub)
         def _():
-            padz[:, 8 : 8 + F] = mb[ph, i].astype(F32) * scale
-            for f in range(6):
-                picks = [chosen(hub_side, hub_nb[f], o) for o in range(3)]
-                shifted = [padz[f, 7 + o : 7 + o + F] for o in range(3)]
-                for k in range(9):
-                    total = jnp.zeros((F, C), F32)
-                    for o in range(3):
-                        total = jnp.where(picks[o] == k, shifted[o], total)
-                    extra[f * F : f * F + F, k * C : k * C + C] = total.astype(BF)
-
-    def spread(dst, extra, weights, width):
-        result = dot(dst[...], weights)
-        field[:, :, 0:width] = result[0:cells].reshape(6, F, width)
-        for f in range(6):
-            field[f, F - 1 : F, 0:width] += result[cells + f : cells + f + 1]
-            field[f, 0:1, 0:width] += result[cells + 8 + f : cells + 9 + f]
-
-        @pl.when(ishub)
-        def _():
-            field[:, :, 0:width] += dot(extra[...], weights).reshape(6, F, width)
-
-        return field[:, :, 0:width].reshape(cells, width)
+            hub_taps(ph, i, extra, scale)
+            ref[:, :, lanes] += dot(extra[...], weights).reshape(6, F, width)
 
     for cp in loads:
         cp.wait()
     prepare(0)
-    base = 2 + 1 + 1 + (ny - 1) + (nz - 1)
+    base = 4 + (ny - 1) + (nz - 1)
     pl.semaphore_wait(barrier, base + 2 + jnp.where(ishub, n - 2, 0))
     send(0)
+    send_rows(0)
 
     padz[...] = jnp.zeros(padz.shape, F32)
     for cp in wloads:
@@ -470,44 +477,52 @@
         c0mat[...] = onehot(((code_a & 3) == hub_side) & (b == other + F - 1 - pos))
         c2mat[...] = onehot(((code_a & 3) == 2 - hub_side) & (b == other + pos))
 
+    inputs = ((0, tu, False, 1.0), (1, tv, False, 1.0), (2, ts, True, 0.5))
+    for i, dst, spreads, scale in inputs:
+        row_taps(0, i, 1, dst, spreads, scale)
     margins(0)
     receive(0, (2,))
 
-    forward_taps(0, 0, tu)
-    forward_taps(0, 1, tv)
-    spread_taps(0, 2, ts, tx, 0.5)
-    joined = dot(tu[...], wf1[...])
-    hidden = joined[:, 0:C]
-    hidden_tangent = joined[:, C : 2 * C] + dot(tv[...], wraw[0])
-    squash = jnp.tanh(hidden)
+    for i, dst, spreads, scale in inputs:
+        row_taps(0, i, 0, dst, spreads, scale)
+        row_taps(0, i, 2, dst, spreads, scale)
+    both = slice(0, 2 * C)
+    left = slice(0, C)
+    right = slice(C, 2 * C)
+    front[...] = dot(tu[0:cells], wf1[...]).reshape(6, F, 2 * C)
+    front[:, :, right] += dot(tv[0:cells], wraw[0]).reshape(6, F, C)
+    main_spread(0, 2, ts, tx, ws2[...], 0.5, field, both)
+    receive_margins(0)
+    forward_sides(0, 0, tu)
+    forward_sides(0, 1, tv)
+    spread_sides(0, 2, ts, 0.5)
+    side = dot(tu[cells:], wf1[...])
+    more = dot(tv[cells:], wraw[0])
+    add_sides(front, both, side)
+    add_sides(front, right, more)
+    add_sides(field, both, dot(ts[cells:], ws2[...]))
+    squash = jnp.tanh(front[:, :, left])
     derivative = 1.0 - squash * squash
-    act = squash.astype(BF)
+    hidden_tangent = front[:, :, right]
     act_tangent = (derivative * hidden_tangent).astype(BF)
-    aext[0:cells, 0:C] = act
-    aext[0:cells, C : 2 * C] = act_tangent
-    sq[...] = squash.reshape(6, F, C)
-    dd[0:cells, 0:C] = (-2.0 * squash * derivative * hidden_tangent)
-    back = spread(ts, tx, ws2[...], 2 * C)
-    squash = sq[...].reshape(cells, C)
-    derivative = 1.0 - squash * squash
-    delta = (derivative * back[:, 0:C]).astype(BF)
-    delta_tangent = (derivative * back[:, C : 2 * C] + dd[...] * back[:, 0:C]).astype(BF)
-    rb[1, 0, 1] = aext[0:cells, 0:C].reshape(6, F, C)
-    rb[1, 1, 1] = delta.reshape(6, F, C)
-    rb[1, 2, 1] = delta_tangent.reshape(6, F, C)
-    prepare(1)
-    send(1)
-
-    pair = jnp.concatenate([delta, delta_tangent], axis=1)
-    first = dot_t(tu[...], pair)
+    backward = field[:, :, left]
+    scaled = derivative * backward
+    rb[1, 0, 1] = squash.astype(BF)
+    rb[1, 1, 1] = scaled.astype(BF)
+    rb[1, 2, 1] = (derivative * field[:, :, right] - 2.0 * squash * scaled * hidden_tangent).astype(BF)
+    aext[0:cells, right] = act_tangent.reshape(cells, C)
+
+    aext[0:cells, left] = rb[1, 0, 1].reshape(cells, C)
+    aext[cells:, left] = edges(1, 0)
+    zero = jnp.zeros((2, C), F32)
+    wide = act_tangent.astype(F32)
+    aext[cells:, right] = jnp.concatenate([wide[:, F - 1], zero, wide[:, 0], zero], axis=0).astype(BF)
+    for i, lanes in ((1, left), (2, right)):
+        pext[0:cells, lanes] = rb[1, i, 1].reshape(cells, C)
+        pext[cells:, lanes] = edges(1, i)
+    first = dot_t(tu[...], pext[...])
     gsum[0:K9] = first[:, 0:C]
-    gsum[2 * K9 : 3 * K9] = first[:, C : 2 * C] + dot_t(tv[...], delta)
-    zero = jnp.zeros((2, C), F32)
-    tangent = aext[0:cells, C : 2 * C].astype(F32).reshape(6, F, C)
-    aext[cells : cells + SIDES, 0:C] = ebuf[1, 0:16]
-    aext[cells : cells + SIDES, C : 2 * C] = jnp.concatenate(
-        [tangent[:, F - 1], zero, tangent[:, 0], zero], axis=0
-    ).astype(BF)
+    gsum[2 * K9 : 3 * K9] = first[:, C : 2 * C] + dot_t(tv[...], pext[:, left])
     second = dot_t(aext[...], ts[...])
     for k in range(9):
         gsum[K9 + k * C : K9 + k * C + C] = second[0:C, k * C : k * C + C]
@@ -519,6 +534,8 @@
         for k in range(9):
             gsum[K9 + k * C : K9 + k * C + C] += more[0:C, k * C : k * C + C]
             gsum[3 * K9 + k * C : 3 * K9 + k * C + C] += more[C : 2 * C, k * C : k * C + C]
+
+    outs = [pltpu.make_async_copy(res.at[i], ref, osem.at[i]) for i, ref in enumerate((next_ref, adj_ref, adt_ref))]
 
     shard, p0, p1, qn = split_rows(ny, nz)
     qoff = p0 + p1 + qn * core
@@ -586,7 +603,9 @@
             p1_copy(d, size, True).start()
 
     by_core(stage)
-    margins(1)
+    prepare(1)
+    send(1)
+    send_rows(1)
 
     def p2_copy(d, size, out):
         q, p = zpeers[d]
@@ -621,18 +640,17 @@
     for d in range(ny - 1):
         q2(d, True).start()
 
-    receive(1, (1, 2))
-    forward_taps(1, 0, tu)
-    change = dot(tu[...], wraw[2])
-    next_ref[...] = (rb[0, 0, 1].astype(F32).reshape(cells, C) + 0.5 * change).astype(BF).reshape(6, F, C)
-
     scale = 1.0 / F
 
     def p3(d, size, off, out):
         q, p = zpeers[d]
         zz = z if out else q
-        ref = out_ref.at[y, zz, pl.ds(off, size)]
-        return ar("p3", q, zz, ref, ref, p)
+        return ar("p3", q, zz, fin_p.at[pl.ds(0, size)], out_ref.at[y, zz, pl.ds(off, size)], p)
+
+    def own_p(size, off):
+        return pltpu.make_async_copy(fin_p.at[pl.ds(0, size)], out_ref.at[y, z, pl.ds(off, size)], osem.at[3])
+
+    own_q = pltpu.make_async_copy(fin_q, out_ref.at[y, z, pl.ds(qoff, qn)], osem.at[4])
 
     def stage(off, size, ooff, osize):
         for d in range(nz - 1):
@@ -641,7 +659,8 @@
         part = pzf[z, 0:size]
         for q, p in zpeers:
             part = part + pzr[q, 0:size].astype(F32)
-        out_ref[y, z, off : off + size] = (part * scale).astype(BF)
+        fin_p[0:size] = (part * scale).astype(BF)
+        own_p(size, off).start()
         for d in range(nz - 1):
             p3(d, size, off, True).start()
 
@@ -650,8 +669,7 @@
     def q3(d, out):
         q, p = ypeers[d]
         qq = y if out else q
-        ref = out_ref.at[qq, z, pl.ds(qoff, qn)]
-        return ar("q3", q, qq, ref, ref, p)
+        return ar("q3", q, qq, fin_q, out_ref.at[qq, z, pl.ds(qoff, qn)], p)
 
     for d in range(ny - 1):
         q2(d, True).wait_send()
@@ -659,14 +677,16 @@
     part = qyf[y]
     for q, p in ypeers:
         part = part + qyr[q].astype(F32)
-    out_ref[y, z, pl.ds(pl.multiple_of(qoff, 16), qn)] = (part * scale).astype(BF)
+    fin_q[...] = (part * scale).astype(BF)
+    own_q.start()
     for d in range(ny - 1):
         q3(d, True).start()
 
-    spread_taps(1, 1, ts, tx, 1.0)
-    back = spread(ts, tx, ws1[...], 2 * C)
-    adj_ref[...] = (rb[0, 2, 1].astype(F32).reshape(cells, C) + back[:, 0:C]).astype(BF).reshape(6, F, C)
-    dd[...] = back[:, C : 2 * C]
+    margins(1)
+    receive(1, (1, 2))
+    for a in range(3):
+        row_taps(1, 0, a, tu, False, 1.0)
+    field[:, :, left] = dot(tu[0:cells], wraw[2]).reshape(6, F, C)
 
     def p4(d, size, off, out):
         q, p = ypeers[d]
@@ -682,6 +702,7 @@
         for d in range(nz - 1):
             p3(d, size, off, True).wait_send()
             p3(d, size, off, False).wait_recv()
+        own_p(size, off).wait()
         for d in range(ny - 1):
             p4(d, size, off, True).start()
         cpy_p(y, size, off).start()
@@ -701,13 +722,31 @@
     for d in range(ny - 1):
         q3(d, True).wait_send()
         q3(d, False).wait_recv()
+    own_q.wait()
     for d in range(nz - 1):
         q4(d, True).start()
     cpy_q(z, qoff).start()
 
-    spread_taps(1, 2, ty, tx, 1.0)
-    back = spread(ty, tx, ws1[:, 0:C], C)
-    adt_ref[...] = (dd[...] + back).astype(BF).reshape(6, F, C)
+    receive_margins(1)
+    forward_sides(1, 0, tu)
+    add_sides(field, left, dot(tu[cells:], wraw[2]))
+    res[0] = (rb[0, 0, 1].astype(F32) + 0.5 * field[:, :, left]).astype(BF)
+    outs[0].start()
+
+    def adjoint_of(i, dst, weights, ref, lanes):
+        for a in range(3):
+            row_taps(1, i, a, dst, True, 1.0)
+        spread_sides(1, i, dst, 1.0)
+        main_spread(1, i, dst, tx, weights, 1.0, ref, lanes)
+        add_sides(ref, lanes, dot(dst[cells:], weights))
+
+    adjoint_of(1, ts, ws1[...], front, both)
+    res[1] = (rb[0, 2, 1].astype(F32) + front[:, :, left]).astype(BF)
+    outs[1].start()
+
+    adjoint_of(2, ts, ws1[:, 0:C], field, left)
+    res[2] = (front[:, :, right] + field[:, :, left]).astype(BF)
+    outs[2].start()
 
     def stage(off, size, ooff, osize):
         for d in range(ny - 1):
@@ -732,6 +771,8 @@
     for q in range(nz):
         cpy_q(q, qoff).wait_send()
         cpy_q(q, qother).wait_recv()
+    for cp in outs:
+        cp.wait()
     finish_sends(0)
     finish_sends(1)
 
@@ -757,6 +798,32 @@
     qn = 2 * tiles // 9
     p1 = (tiles - 2 * qn) // 2
     return 16 * tiles, 16 * (tiles - 2 * qn - p1), 16 * p1, 16 * qn
+
+
+CHUNKS = 8
+
+
+def finish(n_ref, a_ref, t_ref, g_ref, n_out, a_out, t_out, w_out, h_out, packed, wide, held, in_sem, out_sem, row_in, row_out):
+    size = packed.shape[1]
+    row_ins = [pltpu.make_async_copy(src, held.at[i], row_in.at[i]) for i, src in enumerate((n_ref, a_ref, t_ref))]
+    row_outs = [pltpu.make_async_copy(held.at[i], dst, row_out.at[i]) for i, dst in enumerate((n_out, a_out, t_out))]
+    half = CHUNKS // 2
+    ins = [pltpu.make_async_copy(g_ref.at[pl.ds(i * size, size)], packed.at[i], in_sem.at[i]) for i in range(CHUNKS)]
+    outs = [
+        pltpu.make_async_copy(wide.at[i], (w_out, h_out)[i // half].at[pl.ds(i % half * size, size)], out_sem.at[i])
+        for i in range(CHUNKS)
+    ]
+    for cp in ins + row_ins:
+        cp.start()
+    for i in range(CHUNKS):
+        ins[i].wait()
+        wide[i] = packed[i].astype(F32)
+        outs[i].start()
+    for i in range(3):
+        row_ins[i].wait()
+        row_outs[i].start()
+    for cp in outs + row_outs:
+        cp.wait()
 
 
 def on_device(n, ny, nz, u, v, c, w1, w2, t1, t2, nb):
@@ -775,7 +842,7 @@
         functools.partial(kernel, n, ny, nz),
         out_shape=(row, row, row, jax.ShapeDtypeStruct((ny, nz, shard, C), BF)),
         in_specs=[anywhere] * 8,
-        out_specs=(inside,) * 4,
+        out_specs=(anywhere,) * 4,
         scratch_shapes=[
             vm((2, 3, 3, 6, F, C), BF),
             vm((2, 3, 6, F, C), BF),
@@ -795,15 +862,13 @@
             vm((K9, 2 * C), BF),
             vm((K9, 2 * C), BF),
             vm((6, F + 16, C), F32),
-            vm((6, F + 16, C), F32),
-            vm((cells, K9), BF),
-            vm((cells, K9), BF),
+            vm((cells + SIDES, K9), BF),
+            vm((cells + SIDES, K9), BF),
             vm((cells + SIDES, K9), BF),
             vm((cells, K9), BF),
-            vm((cells + SIDES, K9), BF),
-            vm((6, F, C), F32),
             vm((cells + SIDES, 2 * C), BF),
-            vm((cells, C), F32),
+            vm((cells + SIDES, 2 * C), BF),
+            vm((6, F, 2 * C), F32),
             vm((6, F, 2 * C), F32),
             vm((4 * K9, C), F32),
             vm((ny, nz, shard, C), BF),
@@ -820,7 +885,11 @@
             vm((ny, qn, C), BF),
             vm((ny, qn, C), F32),
             vm((ny, qn, C), BF),
-            pltpu.SMEM((6, 4), jnp.int32),
+            pltpu.SMEM((4, 6), jnp.int32),
+            vm((3, 6, F, C), BF),
+            vm((p0, C), BF),
+            vm((qn, C), BF),
+            dma((5,)),
             dma((8,)),
             dma((2, 3, 2)),
             dma((2, 3, 2)),
@@ -838,10 +907,20 @@
         compiler_params=pltpu.CompilerParams(
             collective_id=0, has_side_effects=True, vmem_limit_bytes=56 * 2**20
         ),
-    )(u, v, c, w1, w2, t1, t2, nb)
-    grads = out.reshape(2, 2, 9, C, C).astype(F32)
+    )(u, v, c, w1, w2, t1, t2, nb.T)
+    half = 2 * K9
+    grad = jax.ShapeDtypeStruct((half, C), F32)
+    nxt, adj, adt, wg, hp = pl.pallas_call(
+        finish,
+        out_shape=(row, row, row, grad, grad),
+        in_specs=[anywhere] * 4,
+        out_specs=(anywhere,) * 5,
+        scratch_shapes=[vm((CHUNKS, 2 * half // CHUNKS, C), BF), vm((CHUNKS, 2 * half // CHUNKS, C), F32), vm((3, 6, F, C), BF), dma((CHUNKS,)), dma((CHUNKS,)), dma((3,)), dma((3,))],
+        compiler_params=pltpu.CompilerParams(vmem_limit_bytes=56 * 2**20),
+    )(nxt, adj, adt, out.reshape(2 * half, C))
+    shape4 = (2, 9, C, C)
     shape = (6, 1, F, C)
-    return nxt.reshape(shape), adj.reshape(shape), adt.reshape(shape), grads[0], grads[1]
+    return nxt.reshape(shape), adj.reshape(shape), adt.reshape(shape), wg.reshape(shape4), hp.reshape(shape4)
 
 
 def solution(mesh):

time: 76.7 us -> 69.1 us (0.901)
  local copies, waits for them, and re-layouts: 6.17 us -> 0 us
  Pallas kernels: 69.4 us -> 68 us
    pallas_call x1, Pallas kernels: 69.4 us -> 65.4 us  [on_device(): pl.pallas_call(functools.partial(kernel, n, ny, nz), out_shape=(row, row,...]
    unnamed x10 -> x0, local copies, waits for them, and re-layouts: 3.29 us -> none
    slice x1 -> x0, local copies, waits for them, and re-layouts: 2.89 us -> none  [on_device(): grads[1]]
    pallas_call x0 -> x1, Pallas kernels: none -> 2.61 us  [on_device(): pl.pallas_call(finish, out_shape=(row, row, row, grad, grad), in_specs=[a...]
where the time goes in v3:
time: 69.1 us; the launch traced here: 68.6 us
  Pallas kernels  68 us (98%)
    pallas_call x1, Pallas kernels, on_device(): pl.pallas_call(functools.partial(kernel, n, ny, nz), out_shape=(row, row,...  65.4 us
    pallas_call x1, Pallas kernels, on_device(): pl.pallas_call(finish, out_shape=(row, row, row, grad, grad), in_specs=[a...  2.61 us

profile of v3, /device:TPU:1, one launch (start us, length us, event | category | flops | bytes accessed | tf_op | source)
XLA Modules:
  0.0 68.6 jit_solution(17084672090043800131)
XLA Ops:
  0.6 65.4 %shard_map.119 = (bf16[6,64,128]{2,1,0:T(8,128)(2,1)}, bf16[6,64,128]{2,1,0:T(8,128)(2,1)}, bf16[6,64,128]{2,1,0:T(8,128)(2,1)}, bf16[4,8,144,128]{3,2,1,0:T(8,128)(2,1)}) custom-call(bf16[6,64,128]{2,1,0:T(8,128)(2,1)} %bitcast.25, bf16[6,64,128]{2,1,0:T(8,128)(2,1)} %bitcast.26, bf16[6,64,128]{2,1,0:T(8,128)(2,1)} %bitcast.27, bf16[1152,128]{1,0:T(8,128)(2,1)} %bitcast.21, ...), custom_call_target="tpu_custom_call" | custom-call | tf_op jit(solution)/shard_map/pallas_call | solution.py:841
  66.0 2.6 %shard_map.120 = (bf16[6,64,128]{2,1,0:T(8,128)(2,1)}, bf16[6,64,128]{2,1,0:T(8,128)(2,1)}, bf16[6,64,128]{2,1,0:T(8,128)(2,1)}, f32[2304,128]{1,0:T(8,128)}, f32[2304,128]{1,0:T(8,128)}) custom-call(bf16[6,64,128]{2,1,0:T(8,128)(2,1)} %get-tuple-element.14.n_ref, bf16[6,64,128]{2,1,0:T(8,128)(2,1)} %get-tuple-element.15.a_ref, ...), custom_call_target="tpu_custom_call" | custom-call | tf_op jit(solution)/shard_map/pallas_call | solution.py:913

commit v4 on v3

--- a/solution.py
+++ b/solution.py
@@ -126,6 +126,12 @@
     up = lax.rem(r + n - 1, n)
     dn = lax.rem(r + 1, n)
     mirror = n - 1 - r
+    odd = lax.rem(r, 2)
+    beside = r + 1 - 2 * odd
+    beyond = lax.rem(r + n - 1 + 2 * odd, n)
+    outer = jnp.logical_or(lax.rem(r, 4) == 0, lax.rem(r, 4) == 3)
+    slot_in = 2 - 2 * odd
+    slot_out = 2 * odd
     partner = make(yhi, z, 1 - core, ylo)
 
     def ypeer(d):
@@ -289,19 +295,46 @@
     def z_copy(ph, h, p):
         return rcopy(zs.at[ph, p], ebuf.at[ph, pl.ds(96 + 32 * h, 32)], z_s.at[ph, p], z_r.at[ph, h], p)
 
-    def bulk_copy(ph, i, way):
-        return rcopy(
-            rb.at[ph, i, 1],
-            rb.at[ph, i, 2 if way == 0 else 0],
-            bulk_s.at[ph, i, way],
-            bulk_r.at[ph, i, way],
-            up if way == 0 else dn,
-        )
-
-    def send_rows(ph):
+    def row_beside(ph, i, out):
+        slot = slot_out if out else slot_in
+        return rcopy(rb.at[ph, i, 1], rb.at[ph, i, slot], bulk_s.at[ph, i, 0], bulk_r.at[ph, i, 0], beside)
+
+    def row_beyond(ph, i, out):
+        slot = slot_in if out else slot_out
+        return rcopy(rb.at[ph, i, 1], rb.at[ph, i, slot], bulk_s.at[ph, i, 1], bulk_r.at[ph, i, 1], beyond)
+
+    def row_inward(ph, i):
+        return rcopy(rb.at[ph, i, slot_in], rb.at[ph, i, slot_out], bulk_s.at[ph, i, 2], bulk_r.at[ph, i, 1], partner)
+
+    def send_rows(ph, fields=(0, 1, 2)):
+        for i in fields:
+            row_beside(ph, i, True).start()
+
+            @pl.when(outer)
+            def _():
+                row_beyond(ph, i, True).start()
+
+    def hand_row(ph, i):
+        @pl.when(outer)
+        def _():
+            row_beside(ph, i, False).wait_recv()
+            row_inward(ph, i).start()
+
+    def receive_row(ph, i):
+        @pl.when(jnp.logical_not(outer))
+        def _():
+            row_beside(ph, i, False).wait_recv()
+
+        row_beyond(ph, i, False).wait_recv()
+
+    def finish_rows(ph):
         for i in range(3):
-            for way in range(2):
-                bulk_copy(ph, i, way).start()
+            row_beside(ph, i, True).wait_send()
+
+            @pl.when(outer)
+            def _():
+                row_beyond(ph, i, True).wait_send()
+                row_inward(ph, i).wait_send()
 
     def mt_copy(ph, way):
         return rcopy(
@@ -344,29 +377,25 @@
         for way in range(2):
             mt_copy(ph, way).start()
 
-    def hub_row(ph, spreads):
+    def hub_wait(ph):
         @pl.when(ishub)
         def _():
             hub_loop(lambda p: rcopy(hm.at[ph, pl.ds(0, 32)], rx.at[ph, p], hm_s.at[ph, 0], rx_r.at[ph, p], p).wait_recv())
+
+    def hub_row(ph, i, spreads):
+        @pl.when(ishub)
+        def _():
             slot = jnp.where(is0, 0, 2)
-            got = rx[ph].astype(F32)
-            for i in range(3):
-                piece = got[:, 8 * i : 8 * i + 8].reshape(8 * F, C).astype(BF)
-                row = dot(bmat[...], piece)
-                row = row + dot(c0mat[...], rb[ph, i, 1].reshape(cells, C))
-                row = row + dot(c2mat[...], rb[ph, i, slot].reshape(cells, C))
-                row = row.astype(BF).reshape(6, F, C)
-                if i in spreads:
-                    mb[ph, i] = row
-                    rb[ph, i, slot] = jnp.zeros((6, F, C), BF)
-                else:
-                    rb[ph, i, slot] = row
-
-    def receive(ph, spreads):
-        for i in range(3):
-            for way in range(2):
-                bulk_copy(ph, i, way).wait()
-        hub_row(ph, spreads)
+            piece = rx[ph].astype(F32)[:, 8 * i : 8 * i + 8].reshape(8 * F, C).astype(BF)
+            row = dot(bmat[...], piece)
+            row = row + dot(c0mat[...], rb[ph, i, 1].reshape(cells, C))
+            row = row + dot(c2mat[...], rb[ph, i, slot].reshape(cells, C))
+            row = row.astype(BF).reshape(6, F, C)
+            if spreads:
+                mb[ph, i] = row
+                rb[ph, i, slot] = jnp.zeros((6, F, C), BF)
+            else:
+                rb[ph, i, slot] = row
 
     def receive_margins(ph):
         for way in range(2):
@@ -480,17 +509,27 @@
     inputs = ((0, tu, False, 1.0), (1, tv, False, 1.0), (2, ts, True, 0.5))
     for i, dst, spreads, scale in inputs:
         row_taps(0, i, 1, dst, spreads, scale)
-    margins(0)
-    receive(0, (2,))
-
-    for i, dst, spreads, scale in inputs:
-        row_taps(0, i, 0, dst, spreads, scale)
-        row_taps(0, i, 2, dst, spreads, scale)
     both = slice(0, 2 * C)
     left = slice(0, C)
     right = slice(C, 2 * C)
+
+    def field_rows(i):
+        receive_row(0, i)
+        _, dst, spreads, scale = inputs[i]
+        hub_row(0, i, spreads)
+        row_taps(0, i, 0, dst, spreads, scale)
+        row_taps(0, i, 2, dst, spreads, scale)
+
+    hand_row(0, 0)
+    margins(0)
+    hand_row(0, 1)
+    hub_wait(0)
+    field_rows(0)
     front[...] = dot(tu[0:cells], wf1[...]).reshape(6, F, 2 * C)
+    hand_row(0, 2)
+    field_rows(1)
     front[:, :, right] += dot(tv[0:cells], wraw[0]).reshape(6, F, C)
+    field_rows(2)
     main_spread(0, 2, ts, tx, ws2[...], 0.5, field, both)
     receive_margins(0)
     forward_sides(0, 0, tu)
@@ -512,6 +551,8 @@
     rb[1, 2, 1] = (derivative * field[:, :, right] - 2.0 * squash * scaled * hidden_tangent).astype(BF)
     aext[0:cells, right] = act_tangent.reshape(cells, C)
 
+    send_rows(1, (0,))
+
     aext[0:cells, left] = rb[1, 0, 1].reshape(cells, C)
     aext[cells:, left] = edges(1, 0)
     zero = jnp.zeros((2, C), F32)
@@ -605,7 +646,7 @@
     by_core(stage)
     prepare(1)
     send(1)
-    send_rows(1)
+    send_rows(1, (1, 2))
 
     def p2_copy(d, size, out):
         q, p = zpeers[d]
@@ -682,8 +723,13 @@
     for d in range(ny - 1):
         q3(d, True).start()
 
+    for i in range(3):
+        hand_row(1, i)
     margins(1)
-    receive(1, (1, 2))
+    hub_wait(1)
+    for i in range(3):
+        receive_row(1, i)
+        hub_row(1, i, i > 0)
     for a in range(3):
         row_taps(1, 0, a, tu, False, 1.0)
     field[:, :, left] = dot(tu[0:cells], wraw[2]).reshape(6, F, C)
@@ -773,8 +819,9 @@
         cpy_q(q, qother).wait_recv()
     for cp in outs:
         cp.wait()
-    finish_sends(0)
-    finish_sends(1)
+    for ph in range(2):
+        finish_sends(ph)
+        finish_rows(ph)
 
 
 PHASES = (
@@ -891,7 +938,7 @@
             vm((qn, C), BF),
             dma((5,)),
             dma((8,)),
-            dma((2, 3, 2)),
+            dma((2, 3, 3)),
             dma((2, 3, 2)),
             dma((2,)),
             dma((2,)),

time: 69.1 us -> 62.4 us (0.903)
  Pallas kernels: 68 us -> 61.4 us
    pallas_call x1, Pallas kernels: 65.4 us -> 58.8 us  [on_device(): pl.pallas_call(functools.partial(kernel, n, ny, nz), out_shape=(row, row,...]
where the time goes in v4:
time: 62.4 us; the launch traced here: 62 us
  Pallas kernels  61.4 us (98%)
  between operations  0.64 us (1%)
    pallas_call x1, Pallas kernels, on_device(): pl.pallas_call(functools.partial(kernel, n, ny, nz), out_shape=(row, row,...  58.8 us
    pallas_call x1, Pallas kernels, on_device(): pl.pallas_call(finish, out_shape=(row, row, row, grad, grad), in_specs=[a...  2.61 us

profile of v4, /device:TPU:1, one launch (start us, length us, event | category | flops | bytes accessed | tf_op | source)
XLA Modules:
  0.0 62.0 jit_solution(3976133075142561086)
XLA Ops:
  0.6 58.8 %shard_map.119 = (bf16[6,64,128]{2,1,0:T(8,128)(2,1)}, bf16[6,64,128]{2,1,0:T(8,128)(2,1)}, bf16[6,64,128]{2,1,0:T(8,128)(2,1)}, bf16[4,8,144,128]{3,2,1,0:T(8,128)(2,1)}) custom-call(bf16[6,64,128]{2,1,0:T(8,128)(2,1)} %bitcast.25, bf16[6,64,128]{2,1,0:T(8,128)(2,1)} %bitcast.26, bf16[6,64,128]{2,1,0:T(8,128)(2,1)} %bitcast.27, bf16[1152,128]{1,0:T(8,128)(2,1)} %bitcast.21, ...), custom_call_target="tpu_custom_call" | custom-call | tf_op jit(solution)/shard_map/pallas_call | solution.py:888
  59.4 2.6 %shard_map.120 = (bf16[6,64,128]{2,1,0:T(8,128)(2,1)}, bf16[6,64,128]{2,1,0:T(8,128)(2,1)}, bf16[6,64,128]{2,1,0:T(8,128)(2,1)}, f32[2304,128]{1,0:T(8,128)}, f32[2304,128]{1,0:T(8,128)}) custom-call(bf16[6,64,128]{2,1,0:T(8,128)(2,1)} %get-tuple-element.14.n_ref, bf16[6,64,128]{2,1,0:T(8,128)(2,1)} %get-tuple-element.15.a_ref, ...), custom_call_target="tpu_custom_call" | custom-call | tf_op jit(solution)/shard_map/pallas_call | solution.py:960

commit v5 on v4

--- a/solution.py
+++ b/solution.py
@@ -288,23 +288,23 @@
             hm.at[ph, pl.ds(32 * h, 32)],
             rx.at[ph, r],
             hm_s.at[ph, h],
-            rx_r.at[ph, r],
+            rx_r.at[ph],
             (n - 1) * h,
         )
 
     def z_copy(ph, h, p):
-        return rcopy(zs.at[ph, p], ebuf.at[ph, pl.ds(96 + 32 * h, 32)], z_s.at[ph, p], z_r.at[ph, h], p)
+        return rcopy(zs.at[ph, p], ebuf.at[ph, pl.ds(96 + 32 * h, 32)], z_s.at[ph], z_r.at[ph, h], p)
 
     def row_beside(ph, i, out):
         slot = slot_out if out else slot_in
-        return rcopy(rb.at[ph, i, 1], rb.at[ph, i, slot], bulk_s.at[ph, i, 0], bulk_r.at[ph, i, 0], beside)
+        return rcopy(rb.at[ph, i, 1], rb.at[ph, i, slot], bulk_s.at[ph, 0], bulk_r.at[ph, i, 0], beside)
 
     def row_beyond(ph, i, out):
         slot = slot_in if out else slot_out
-        return rcopy(rb.at[ph, i, 1], rb.at[ph, i, slot], bulk_s.at[ph, i, 1], bulk_r.at[ph, i, 1], beyond)
+        return rcopy(rb.at[ph, i, 1], rb.at[ph, i, slot], bulk_s.at[ph, 1], bulk_r.at[ph, i, 1], beyond)
 
     def row_inward(ph, i):
-        return rcopy(rb.at[ph, i, slot_in], rb.at[ph, i, slot_out], bulk_s.at[ph, i, 2], bulk_r.at[ph, i, 1], partner)
+        return rcopy(rb.at[ph, i, slot_in], rb.at[ph, i, slot_out], bulk_s.at[ph, 2], bulk_r.at[ph, i, 1], partner)
 
     def send_rows(ph, fields=(0, 1, 2)):
         for i in fields:
@@ -328,13 +328,17 @@
         row_beyond(ph, i, False).wait_recv()
 
     def finish_rows(ph):
-        for i in range(3):
-            row_beside(ph, i, True).wait_send()
-
-            @pl.when(outer)
-            def _():
-                row_beyond(ph, i, True).wait_send()
-                row_inward(ph, i).wait_send()
+        three = rb.at[ph, :, 1]
+
+        def sent(kind):
+            rcopy(three, three, bulk_s.at[ph, kind], bulk_r.at[ph, 0, 0], beside).wait_send()
+
+        sent(0)
+
+        @pl.when(outer)
+        def _():
+            sent(1)
+            sent(2)
 
     def mt_copy(ph, way):
         return rcopy(
@@ -380,7 +384,8 @@
     def hub_wait(ph):
         @pl.when(ishub)
         def _():
-            hub_loop(lambda p: rcopy(hm.at[ph, pl.ds(0, 32)], rx.at[ph, p], hm_s.at[ph, 0], rx_r.at[ph, p], p).wait_recv())
+            start = jnp.where(is0, 1, 0)
+            rcopy(zs.at[ph, pl.ds(0, n - 1)], rx.at[ph, pl.ds(start, n - 1)], z_s.at[ph], rx_r.at[ph], mirror).wait_recv()
 
     def hub_row(ph, i, spreads):
         @pl.when(ishub)
@@ -414,7 +419,7 @@
 
             @pl.when(here)
             def _():
-                hub_loop(lambda p: z_copy(ph, h, p).wait_send())
+                rcopy(zs.at[ph, pl.ds(0, n - 1)], rx.at[ph, pl.ds(0, n - 1)], z_s.at[ph], rx_r.at[ph], mirror).wait_send()
 
             @pl.when(jnp.logical_not(here))
             def _():
@@ -581,10 +586,6 @@
     shard, p0, p1, qn = split_rows(ny, nz)
     qoff = p0 + p1 + qn * core
     qother = p0 + p1 + qn * (1 - core)
-    slots = {}
-    for name, count in PHASES:
-        slots[name] = sum(ny if c == "y" else nz if c == "z" else 1 for _, c in PHASES[: len(slots)])
-
     def by_core(fn):
         @pl.when(core == 0)
         def _():
@@ -594,8 +595,15 @@
         def _():
             fn(p0, p1, 0, p0)
 
-    def ar(name, slot_s, slot_r, src, dst, p):
-        return rcopy(src, dst, ar_s.at[slots[name] + slot_s], ar_r.at[slots[name] + slot_r], p)
+    def ar(name, src, dst, p, extra=None):
+        at = STEPS.index(name)
+        return rcopy(src, dst, ar_s.at[at], ar_r.at[at if extra is None else len(STEPS) + extra], p)
+
+    def sent(name, src):
+        ar(name, src, src, partner).wait_send()
+
+    def arrived(name, dst):
+        ar(name, dst, dst, partner).wait_recv()
 
     ypeers = [ypeer(d) for d in range(1, ny)]
     zpeers = [zpeer(d) for d in range(1, nz)]
@@ -603,24 +611,24 @@
     gs[...] = whole.astype(BF)
 
     def core_p(off, size, ooff, osize):
-        return ar("cp", 0, 0, gs.at[:, :, pl.ds(ooff, osize)], gr.at[:, :, pl.ds(ooff, osize)], partner)
+        return ar("cp", gs.at[:, :, pl.ds(ooff, osize)], gr.at[:, :, pl.ds(ooff, osize)], partner)
 
     def core_p_in(off, size, ooff, osize):
-        return ar("cp", 0, 0, gs.at[:, :, pl.ds(off, size)], gr.at[:, :, pl.ds(off, size)], partner)
+        return ar("cp", gs.at[:, :, pl.ds(off, size)], gr.at[:, :, pl.ds(off, size)], partner)
 
     def core_q(o):
-        return ar("cq", 0, 0, gs.at[:, :, pl.ds(o, qn)], gr.at[:, :, pl.ds(o, qn)], partner)
+        return ar("cq", gs.at[:, :, pl.ds(o, qn)], gr.at[:, :, pl.ds(o, qn)], partner)
 
     core_q(qother).start()
     by_core(lambda *a: core_p(*a).start())
 
-    def q1(d, out):
+    def q1(d):
         q, p = zpeers[d]
-        return ar("q1", q, z if out else q, qs.at[:, q], qr.at[z if out else q], p)
-
-    def p1_copy(d, size, out):
+        return ar("q1", qs.at[:, q], qr.at[z], p)
+
+    def p1_copy(d, size):
         q, p = ypeers[d]
-        return ar("p1", q, y if out else q, ps.at[q, :, pl.ds(0, size)], pr.at[y if out else q, :, pl.ds(0, size)], p)
+        return ar("p1", ps.at[q, :, pl.ds(0, size)], pr.at[y, :, pl.ds(0, size)], p)
 
     core_q(qother).wait_send()
     core_q(qoff).wait_recv()
@@ -632,7 +640,7 @@
 
     by_core(lambda off, size, ooff, osize: stage(p0 + p1 if off == 0 else p0 + p1 + qn))
     for d in range(nz - 1):
-        q1(d, True).start()
+        q1(d).start()
 
     def stage(off, size, ooff, osize):
         core_p(off, size, ooff, osize).wait_send()
@@ -641,52 +649,47 @@
         pf[:, :, 0:size] = part
         ps[:, :, 0:size] = part.astype(BF)
         for d in range(ny - 1):
-            p1_copy(d, size, True).start()
+            p1_copy(d, size).start()
 
     by_core(stage)
     prepare(1)
     send(1)
     send_rows(1, (1, 2))
 
-    def p2_copy(d, size, out):
+    def p2_copy(d, size):
         q, p = zpeers[d]
-        return ar("p2", q, z if out else q, pz.at[q, pl.ds(0, size)], pzr.at[z if out else q, pl.ds(0, size)], p)
+        return ar("p2", pz.at[q, pl.ds(0, size)], pzr.at[z, pl.ds(0, size)], p)
 
     def stage(off, size, ooff, osize):
-        for d in range(ny - 1):
-            p1_copy(d, size, True).wait_send()
-            p1_copy(d, size, False).wait_recv()
+        arrived("p1", pr.at[pl.ds(0, ny - 1), :, pl.ds(0, size)])
         part = pf[y, :, 0:size]
         for q, p in ypeers:
             part = part + pr[q, :, 0:size].astype(F32)
         pzf[:, 0:size] = part
         pz[:, 0:size] = part.astype(BF)
         for d in range(nz - 1):
-            p2_copy(d, size, True).start()
+            p2_copy(d, size).start()
 
     by_core(stage)
 
-    def q2(d, out):
+    def q2(d):
         q, p = ypeers[d]
-        return ar("q2", q, y if out else q, qy.at[q], qyr.at[y if out else q], p)
-
-    for d in range(nz - 1):
-        q1(d, True).wait_send()
-        q1(d, False).wait_recv()
+        return ar("q2", qy.at[q], qyr.at[y], p)
+
+    arrived("q1", qr.at[pl.ds(0, nz - 1)])
     part = qf[:, z]
     for q, p in zpeers:
         part = part + qr[q].astype(F32)
     qyf[...] = part
     qy[...] = part.astype(BF)
     for d in range(ny - 1):
-        q2(d, True).start()
+        q2(d).start()
 
     scale = 1.0 / F
 
-    def p3(d, size, off, out):
+    def p3(d, size, off):
         q, p = zpeers[d]
-        zz = z if out else q
-        return ar("p3", q, zz, fin_p.at[pl.ds(0, size)], out_ref.at[y, zz, pl.ds(off, size)], p)
+        return ar("p3", fin_p.at[pl.ds(0, size)], out_ref.at[y, z, pl.ds(off, size)], p)
 
     def own_p(size, off):
         return pltpu.make_async_copy(fin_p.at[pl.ds(0, size)], out_ref.at[y, z, pl.ds(off, size)], osem.at[3])
@@ -694,34 +697,29 @@
     own_q = pltpu.make_async_copy(fin_q, out_ref.at[y, z, pl.ds(qoff, qn)], osem.at[4])
 
     def stage(off, size, ooff, osize):
-        for d in range(nz - 1):
-            p2_copy(d, size, True).wait_send()
-            p2_copy(d, size, False).wait_recv()
+        arrived("p2", pzr.at[pl.ds(0, nz - 1), pl.ds(0, size)])
         part = pzf[z, 0:size]
         for q, p in zpeers:
             part = part + pzr[q, 0:size].astype(F32)
         fin_p[0:size] = (part * scale).astype(BF)
         own_p(size, off).start()
         for d in range(nz - 1):
-            p3(d, size, off, True).start()
+            p3(d, size, off).start()
 
     by_core(stage)
 
-    def q3(d, out):
+    def q3(d):
         q, p = ypeers[d]
-        qq = y if out else q
-        return ar("q3", q, qq, fin_q, out_ref.at[qq, z, pl.ds(qoff, qn)], p)
-
-    for d in range(ny - 1):
-        q2(d, True).wait_send()
-        q2(d, False).wait_recv()
+        return ar("q3", fin_q, out_ref.at[y, z, pl.ds(qoff, qn)], p)
+
+    arrived("q2", qyr.at[pl.ds(0, ny - 1)])
     part = qyf[y]
     for q, p in ypeers:
         part = part + qyr[q].astype(F32)
     fin_q[...] = (part * scale).astype(BF)
     own_q.start()
     for d in range(ny - 1):
-        q3(d, True).start()
+        q3(d).start()
 
     for i in range(3):
         hand_row(1, i)
@@ -738,16 +736,14 @@
         q, p = ypeers[d]
         qq = y if out else q
         ref = out_ref.at[qq, :, pl.ds(off, size)]
-        return ar("p4", q, qq, ref, ref, p)
+        return ar("p4", ref, ref, p, qq)
 
     def cpy_p(q, size, off):
         ref = out_ref.at[q, :, pl.ds(off, size)]
-        return ar("c4", q, q, ref, ref, partner)
+        return ar("c4", ref, ref, partner)
 
     def stage(off, size, ooff, osize):
-        for d in range(nz - 1):
-            p3(d, size, off, True).wait_send()
-            p3(d, size, off, False).wait_recv()
+        arrived("p3", out_ref.at[y, pl.ds(0, nz - 1), pl.ds(off, size)])
         own_p(size, off).wait()
         for d in range(ny - 1):
             p4(d, size, off, True).start()
@@ -759,15 +755,13 @@
         q, p = zpeers[d]
         qq = z if out else q
         ref = out_ref.at[:, qq, pl.ds(qoff, qn)]
-        return ar("q4", q, qq, ref, ref, p)
+        return ar("q4", ref, ref, p, ny + qq)
 
     def cpy_q(q, o):
         ref = out_ref.at[:, q, pl.ds(o, qn)]
-        return ar("d4", q, q, ref, ref, partner)
-
-    for d in range(ny - 1):
-        q3(d, True).wait_send()
-        q3(d, False).wait_recv()
+        return ar("d4", ref, ref, partner)
+
+    arrived("q3", out_ref.at[pl.ds(0, ny - 1), z, pl.ds(qoff, qn)])
     own_q.wait()
     for d in range(nz - 1):
         q4(d, True).start()
@@ -805,18 +799,20 @@
         cpy_q(zpeers[d][0], qoff).start()
 
     def stage(off, size, ooff, osize):
-        for d in range(ny - 1):
-            p4(d, size, off, True).wait_send()
-        for q in range(ny):
-            cpy_p(q, size, off).wait_send()
-            cpy_p(q, osize, ooff).wait_recv()
+        sent("p1", pr.at[pl.ds(0, ny - 1), :, pl.ds(0, size)])
+        sent("p2", pzr.at[pl.ds(0, nz - 1), pl.ds(0, size)])
+        sent("p3", out_ref.at[y, pl.ds(0, nz - 1), pl.ds(off, size)])
+        sent("p4", out_ref.at[pl.ds(0, ny - 1), :, pl.ds(off, size)])
+        sent("c4", out_ref.at[:, :, pl.ds(off, size)])
+        arrived("c4", out_ref.at[:, :, pl.ds(ooff, osize)])
 
     by_core(stage)
-    for d in range(nz - 1):
-        q4(d, True).wait_send()
-    for q in range(nz):
-        cpy_q(q, qoff).wait_send()
-        cpy_q(q, qother).wait_recv()
+    sent("q1", qr.at[pl.ds(0, nz - 1)])
+    sent("q2", qyr.at[pl.ds(0, ny - 1)])
+    sent("q3", out_ref.at[pl.ds(0, ny - 1), z, pl.ds(qoff, qn)])
+    sent("q4", out_ref.at[:, pl.ds(0, nz - 1), pl.ds(qoff, qn)])
+    sent("d4", out_ref.at[:, :, pl.ds(qoff, qn)])
+    arrived("d4", out_ref.at[:, :, pl.ds(qother, qn)])
     for cp in outs:
         cp.wait()
     for ph in range(2):
@@ -824,20 +820,7 @@
         finish_rows(ph)
 
 
-PHASES = (
-    ("cp", "1"),
-    ("cq", "1"),
-    ("q1", "z"),
-    ("p1", "y"),
-    ("p2", "z"),
-    ("q2", "y"),
-    ("p3", "z"),
-    ("q3", "y"),
-    ("p4", "y"),
-    ("c4", "y"),
-    ("q4", "z"),
-    ("d4", "z"),
-)
+STEPS = ("cp", "cq", "q1", "p1", "p2", "q2", "p3", "q3", "p4", "c4", "q4", "d4")
 
 
 def split_rows(ny, nz):
@@ -877,7 +860,6 @@
     F = n
     cells = 6 * F
     shard, p0, p1, qn = split_rows(ny, nz)
-    arrived = sum(ny if c == "y" else nz if c == "z" else 1 for _, c in PHASES)
     u, v, c = (a.reshape(6, F, C) for a in (u, v, c))
     w1, w2, t1, t2 = (a.reshape(K9, C) for a in (w1, w2, t1, t2))
     vm = pltpu.VMEM
@@ -938,18 +920,18 @@
             vm((qn, C), BF),
             dma((5,)),
             dma((8,)),
-            dma((2, 3, 3)),
+            dma((2, 3)),
             dma((2, 3, 2)),
             dma((2,)),
             dma((2,)),
             dma((2, 2)),
-            dma((2, n)),
-            dma((2, n)),
+            dma((2,)),
+            dma((2,)),
             dma((2, 2)),
             dma((2, 2)),
             dma((2, 2)),
-            dma((arrived,)),
-            dma((arrived,)),
+            dma((len(STEPS),)),
+            dma((len(STEPS) + ny + nz,)),
         ],
         compiler_params=pltpu.CompilerParams(
             collective_id=0, has_side_effects=True, vmem_limit_bytes=56 * 2**20

time: 62.4 us -> 58.9 us (0.944)
  Pallas kernels: 61.4 us -> 58.1 us
    pallas_call x1, Pallas kernels: 58.8 us -> 55.5 us  [on_device(): pl.pallas_call(functools.partial(kernel, n, ny, nz), out_shape=(row, row,...]
where the time goes in v5:
time: 58.9 us; the launch traced here: 58.8 us
  Pallas kernels  58.1 us (99%)
  between operations  0.64 us (1%)
    pallas_call x1, Pallas kernels, on_device(): pl.pallas_call(functools.partial(kernel, n, ny, nz), out_shape=(row, row,...  55.5 us
    pallas_call x1, Pallas kernels, on_device(): pl.pallas_call(finish, out_shape=(row, row, row, grad, grad), in_specs=[a...  2.61 us

profile of v5, /device:TPU:1, one launch (start us, length us, event | category | flops | bytes accessed | tf_op | source)
XLA Modules:
  0.0 58.8 jit_solution(475238333215323778)
XLA Ops:
  0.6 55.5 %shard_map.119 = (bf16[6,64,128]{2,1,0:T(8,128)(2,1)}, bf16[6,64,128]{2,1,0:T(8,128)(2,1)}, bf16[6,64,128]{2,1,0:T(8,128)(2,1)}, bf16[4,8,144,128]{3,2,1,0:T(8,128)(2,1)}) custom-call(bf16[6,64,128]{2,1,0:T(8,128)(2,1)} %bitcast.25, bf16[6,64,128]{2,1,0:T(8,128)(2,1)} %bitcast.26, bf16[6,64,128]{2,1,0:T(8,128)(2,1)} %bitcast.27, bf16[1152,128]{1,0:T(8,128)(2,1)} %bitcast.21, ...), custom_call_target="tpu_custom_call" | custom-call | tf_op jit(solution)/shard_map/pallas_call | solution.py:870
  56.2 2.6 %shard_map.120 = (bf16[6,64,128]{2,1,0:T(8,128)(2,1)}, bf16[6,64,128]{2,1,0:T(8,128)(2,1)}, bf16[6,64,128]{2,1,0:T(8,128)(2,1)}, f32[2304,128]{1,0:T(8,128)}, f32[2304,128]{1,0:T(8,128)}) custom-call(bf16[6,64,128]{2,1,0:T(8,128)(2,1)} %get-tuple-element.14.n_ref, bf16[6,64,128]{2,1,0:T(8,128)(2,1)} %get-tuple-element.15.a_ref, ...), custom_call_target="tpu_custom_call" | custom-call | tf_op jit(solution)/shard_map/pallas_call | solution.py:942

commit v6 on v5

--- a/solution.py
+++ b/solution.py
@@ -558,30 +558,25 @@
 
     send_rows(1, (0,))
 
+    prepare(1)
+    send(1)
+
     aext[0:cells, left] = rb[1, 0, 1].reshape(cells, C)
     aext[cells:, left] = edges(1, 0)
     zero = jnp.zeros((2, C), F32)
     wide = act_tangent.astype(F32)
     aext[cells:, right] = jnp.concatenate([wide[:, F - 1], zero, wide[:, 0], zero], axis=0).astype(BF)
-    for i, lanes in ((1, left), (2, right)):
-        pext[0:cells, lanes] = rb[1, i, 1].reshape(cells, C)
-        pext[cells:, lanes] = edges(1, i)
-    first = dot_t(tu[...], pext[...])
-    gsum[0:K9] = first[:, 0:C]
-    gsum[2 * K9 : 3 * K9] = first[:, C : 2 * C] + dot_t(tv[...], pext[:, left])
     second = dot_t(aext[...], ts[...])
     for k in range(9):
-        gsum[K9 + k * C : K9 + k * C + C] = second[0:C, k * C : k * C + C]
-        gsum[3 * K9 + k * C : 3 * K9 + k * C + C] = second[C : 2 * C, k * C : k * C + C]
+        gsum[k * C : k * C + C] = second[0:C, k * C : k * C + C]
+        gsum[K9 + k * C : K9 + k * C + C] = second[C : 2 * C, k * C : k * C + C]
 
     @pl.when(ishub)
     def _():
         more = dot_t(aext[0:cells], tx[...])
         for k in range(9):
-            gsum[K9 + k * C : K9 + k * C + C] += more[0:C, k * C : k * C + C]
-            gsum[3 * K9 + k * C : 3 * K9 + k * C + C] += more[C : 2 * C, k * C : k * C + C]
-
-    outs = [pltpu.make_async_copy(res.at[i], ref, osem.at[i]) for i, ref in enumerate((next_ref, adj_ref, adt_ref))]
+            gsum[k * C : k * C + C] += more[0:C, k * C : k * C + C]
+            gsum[K9 + k * C : K9 + k * C + C] += more[C : 2 * C, k * C : k * C + C]
 
     shard, p0, p1, qn = split_rows(ny, nz)
     qoff = p0 + p1 + qn * core
@@ -605,56 +600,78 @@
     def arrived(name, dst):
         ar(name, dst, dst, partner).wait_recv()
 
-    ypeers = [ypeer(d) for d in range(1, ny)]
-    zpeers = [zpeer(d) for d in range(1, nz)]
-    whole = gsum[...].reshape(ny, nz, shard, C)
-    gs[...] = whole.astype(BF)
-
-    def core_p(off, size, ooff, osize):
-        return ar("cp", gs.at[:, :, pl.ds(ooff, osize)], gr.at[:, :, pl.ds(ooff, osize)], partner)
-
-    def core_p_in(off, size, ooff, osize):
-        return ar("cp", gs.at[:, :, pl.ds(off, size)], gr.at[:, :, pl.ds(off, size)], partner)
-
-    def core_q(o):
-        return ar("cq", gs.at[:, :, pl.ds(o, qn)], gr.at[:, :, pl.ds(o, qn)], partner)
-
-    core_q(qother).start()
-    by_core(lambda *a: core_p(*a).start())
-
-    def q1(d):
+    ypeers = [ypeer(d) for d in sorted(range(1, ny), key=lambda d: -min(d, ny - d))]
+    zpeers = [zpeer(d) for d in sorted(range(1, nz), key=lambda d: -min(d, nz - d))]
+    hy = ny // 2
+
+    def rows_of(h):
+        return pl.ds(h * hy, hy)
+
+    def core_p(h, off, size):
+        at = (rows_of(h), slice(None), pl.ds(off, size))
+        return ar(("cp0", "cp1")[h], gs.at[at], gr.at[at], partner)
+
+    def core_q(h, o):
+        at = (rows_of(h), slice(None), pl.ds(o, qn))
+        return ar(("cq0", "cq1")[h], gs.at[at], gr.at[at], partner)
+
+    def swap_cores(h):
+        half = gsum[h * 2 * K9 : (h + 1) * 2 * K9]
+        gs[h * hy : (h + 1) * hy] = half.astype(BF).reshape(hy, nz, shard, C)
+        core_q(h, qother).start()
+        by_core(lambda off, size, ooff, osize: core_p(h, ooff, osize).start())
+
+    def own_half(h, off, size):
+        half = gsum[h * 2 * K9 : (h + 1) * 2 * K9].reshape(hy, nz, shard, C)
+        return half[:, :, off : off + size] + gr[h * hy : (h + 1) * hy, :, off : off + size].astype(F32)
+
+    def q1(h, d):
         q, p = zpeers[d]
-        return ar("q1", qs.at[:, q], qr.at[z], p)
+        return ar("q1", qs.at[rows_of(h), q], qr.at[z, rows_of(h)], p)
 
     def p1_copy(d, size):
         q, p = ypeers[d]
         return ar("p1", ps.at[q, :, pl.ds(0, size)], pr.at[y, :, pl.ds(0, size)], p)
 
-    core_q(qother).wait_send()
-    core_q(qoff).wait_recv()
-
-    def stage(qo):
-        part = gsum[...].reshape(ny, nz, shard, C)[:, :, qo : qo + qn] + gr[:, :, qo : qo + qn].astype(F32)
-        qf[...] = part
-        qs[...] = part.astype(BF)
-
-    by_core(lambda off, size, ooff, osize: stage(p0 + p1 if off == 0 else p0 + p1 + qn))
-    for d in range(nz - 1):
-        q1(d).start()
-
-    def stage(off, size, ooff, osize):
-        core_p(off, size, ooff, osize).wait_send()
-        core_p_in(off, size, ooff, osize).wait_recv()
-        part = gsum[...].reshape(ny, nz, shard, C)[:, :, off : off + size] + gr[:, :, off : off + size].astype(F32)
-        pf[:, :, 0:size] = part
-        ps[:, :, 0:size] = part.astype(BF)
-        for d in range(ny - 1):
-            p1_copy(d, size).start()
-
-    by_core(stage)
-    prepare(1)
-    send(1)
-    send_rows(1, (1, 2))
+    def first_step(h):
+        rows = slice(h * hy, (h + 1) * hy)
+        core_q(h, qother).wait_send()
+        core_q(h, qoff).wait_recv()
+
+        def stage(qo):
+            part = own_half(h, qo, qn)
+            qf[rows] = part
+            qs[rows] = part.astype(BF)
+
+        by_core(lambda off, size, ooff, osize: stage(p0 + p1 if off == 0 else p0 + p1 + qn))
+        for d in range(nz - 1):
+            q1(h, d).start()
+
+        def stage(off, size, ooff, osize):
+            core_p(h, ooff, osize).wait_send()
+            core_p(h, off, size).wait_recv()
+            part = own_half(h, off, size)
+            pf[rows, :, 0:size] = part
+            ps[rows, :, 0:size] = part.astype(BF)
+            for d in range(ny - 1):
+
+                @pl.when(lax.div(ypeers[d][0], hy) == h)
+                def _():
+                    p1_copy(d, size).start()
+
+        by_core(stage)
+
+    swap_cores(0)
+    for i, lanes in ((1, left), (2, right)):
+        pext[0:cells, lanes] = rb[1, i, 1].reshape(cells, C)
+        pext[cells:, lanes] = edges(1, i)
+    first = dot_t(tu[...], pext[...])
+    gsum[2 * K9 : 3 * K9] = first[:, 0:C]
+    gsum[3 * K9 : 4 * K9] = first[:, C : 2 * C] + dot_t(tv[...], pext[:, left])
+    swap_cores(1)
+    first_step(0)
+    first_step(1)
+    send_rows(1, (1,))
 
     def p2_copy(d, size):
         q, p = zpeers[d]
@@ -676,6 +693,7 @@
         q, p = ypeers[d]
         return ar("q2", qy.at[q], qyr.at[y], p)
 
+    send_rows(1, (2,))
     arrived("q1", qr.at[pl.ds(0, nz - 1)])
     part = qf[:, z]
     for q, p in zpeers:
@@ -720,6 +738,10 @@
     own_q.start()
     for d in range(ny - 1):
         q3(d).start()
+    for q, p in zpeers:
+        ar("q4", fin_q, out_ref.at[y, z, pl.ds(qoff, qn)], p, ny + z).start()
+
+    outs = [pltpu.make_async_copy(res.at[i], ref, osem.at[i]) for i, ref in enumerate((next_ref, adj_ref, adt_ref))]
 
     for i in range(3):
         hand_row(1, i)
@@ -751,11 +773,13 @@
 
     by_core(stage)
 
-    def q4(d, out):
-        q, p = zpeers[d]
-        qq = z if out else q
-        ref = out_ref.at[:, qq, pl.ds(qoff, qn)]
-        return ar("q4", ref, ref, p, ny + qq)
+    def q4_in(q):
+        ref = out_ref.at[:, q, pl.ds(qoff, qn)]
+        return ar("q4", ref, ref, partner, ny + q)
+
+    def q4_rest(d, qq):
+        ref = out_ref.at[qq, z, pl.ds(qoff, qn)]
+        return ar("q4", ref, ref, zpeers[d][1], ny + z)
 
     def cpy_q(q, o):
         ref = out_ref.at[:, q, pl.ds(o, qn)]
@@ -764,7 +788,8 @@
     arrived("q3", out_ref.at[pl.ds(0, ny - 1), z, pl.ds(qoff, qn)])
     own_q.wait()
     for d in range(nz - 1):
-        q4(d, True).start()
+        for q, p in ypeers:
+            q4_rest(d, q).start()
     cpy_q(z, qoff).start()
 
     receive_margins(1)
@@ -795,7 +820,7 @@
 
     by_core(stage)
     for d in range(nz - 1):
-        q4(d, False).wait_recv()
+        q4_in(zpeers[d][0]).wait_recv()
         cpy_q(zpeers[d][0], qoff).start()
 
     def stage(off, size, ooff, osize):
@@ -820,7 +845,7 @@
         finish_rows(ph)
 
 
-STEPS = ("cp", "cq", "q1", "p1", "p2", "q2", "p3", "q3", "p4", "c4", "q4", "d4")
+STEPS = ("cp0", "cq0", "cp1", "cq1", "q1", "p1", "p2", "q2", "p3", "q3", "p4", "c4", "q4", "d4")
 
 
 def split_rows(ny, nz):
@@ -837,10 +862,14 @@
     size = packed.shape[1]
     row_ins = [pltpu.make_async_copy(src, held.at[i], row_in.at[i]) for i, src in enumerate((n_ref, a_ref, t_ref))]
     row_outs = [pltpu.make_async_copy(held.at[i], dst, row_out.at[i]) for i, dst in enumerate((n_out, a_out, t_out))]
-    half = CHUNKS // 2
+    quarter = CHUNKS // 4
     ins = [pltpu.make_async_copy(g_ref.at[pl.ds(i * size, size)], packed.at[i], in_sem.at[i]) for i in range(CHUNKS)]
     outs = [
-        pltpu.make_async_copy(wide.at[i], (w_out, h_out)[i // half].at[pl.ds(i % half * size, size)], out_sem.at[i])
+        pltpu.make_async_copy(
+            wide.at[i],
+            (w_out, h_out)[i // quarter % 2].at[pl.ds((i % quarter + (quarter if i < 2 * quarter else 0)) * size, size)],
+            out_sem.at[i],
+        )
         for i in range(CHUNKS)
     ]
     for cp in ins + row_ins:

time: 58.9 us -> 56.6 us (0.961)
  Pallas kernels: 58.1 us -> 55.8 us
    pallas_call x1, Pallas kernels: 55.5 us -> 53.2 us  [on_device(): pl.pallas_call(functools.partial(kernel, n, ny, nz), out_shape=(row, row,...]
where the time goes in v6:
time: 56.6 us; the launch traced here: 56.5 us
  Pallas kernels  55.8 us (99%)
  between operations  0.64 us (1%)
    pallas_call x1, Pallas kernels, on_device(): pl.pallas_call(functools.partial(kernel, n, ny, nz), out_shape=(row, row,...  53.2 us
    pallas_call x1, Pallas kernels, on_device(): pl.pallas_call(finish, out_shape=(row, row, row, grad, grad), in_specs=[a...  2.61 us

profile of v6, /device:TPU:1, one launch (start us, length us, event | category | flops | bytes accessed | tf_op | source)
XLA Modules:
  0.0 56.5 jit_solution(17968142901126949955)
XLA Ops:
  0.6 53.2 %shard_map.119 = (bf16[6,64,128]{2,1,0:T(8,128)(2,1)}, bf16[6,64,128]{2,1,0:T(8,128)(2,1)}, bf16[6,64,128]{2,1,0:T(8,128)(2,1)}, bf16[4,8,144,128]{3,2,1,0:T(8,128)(2,1)}) custom-call(bf16[6,64,128]{2,1,0:T(8,128)(2,1)} %bitcast.25, bf16[6,64,128]{2,1,0:T(8,128)(2,1)} %bitcast.26, bf16[6,64,128]{2,1,0:T(8,128)(2,1)} %bitcast.27, bf16[1152,128]{1,0:T(8,128)(2,1)} %bitcast.21, ...), custom_call_target="tpu_custom_call" | custom-call | tf_op jit(solution)/shard_map/pallas_call | solution.py:899
  53.9 2.6 %shard_map.120 = (bf16[6,64,128]{2,1,0:T(8,128)(2,1)}, bf16[6,64,128]{2,1,0:T(8,128)(2,1)}, bf16[6,64,128]{2,1,0:T(8,128)(2,1)}, f32[2304,128]{1,0:T(8,128)}, f32[2304,128]{1,0:T(8,128)}) custom-call(bf16[6,64,128]{2,1,0:T(8,128)(2,1)} %get-tuple-element.14.n_ref, bf16[6,64,128]{2,1,0:T(8,128)(2,1)} %get-tuple-element.15.a_ref, ...), custom_call_target="tpu_custom_call" | custom-call | tf_op jit(solution)/shard_map/pallas_call | solution.py:971

commit v7 on v6

--- a/solution.py
+++ b/solution.py
@@ -558,9 +558,6 @@
 
     send_rows(1, (0,))
 
-    prepare(1)
-    send(1)
-
     aext[0:cells, left] = rb[1, 0, 1].reshape(cells, C)
     aext[cells:, left] = edges(1, 0)
     zero = jnp.zeros((2, C), F32)
@@ -671,6 +668,8 @@
     swap_cores(1)
     first_step(0)
     first_step(1)
+    prepare(1)
+    send(1)
     send_rows(1, (1,))
 
     def p2_copy(d, size):
@@ -693,7 +692,6 @@
         q, p = ypeers[d]
         return ar("q2", qy.at[q], qyr.at[y], p)
 
-    send_rows(1, (2,))
     arrived("q1", qr.at[pl.ds(0, nz - 1)])
     part = qf[:, z]
     for q, p in zpeers:
@@ -702,6 +700,7 @@
     qy[...] = part.astype(BF)
     for d in range(ny - 1):
         q2(d).start()
+    send_rows(1, (2,))
 
     scale = 1.0 / F
 

time: 56.6 us -> 55.4 us (0.979)
  Pallas kernels: 55.8 us -> 54.6 us
    pallas_call x1, Pallas kernels: 53.2 us -> 52 us  [on_device(): pl.pallas_call(functools.partial(kernel, n, ny, nz), out_shape=(row, row,...]
where the time goes in v7:
time: 55.4 us; the launch traced here: 55.3 us
  Pallas kernels  54.6 us (99%)
  between operations  0.64 us (1%)
    pallas_call x1, Pallas kernels, on_device(): pl.pallas_call(functools.partial(kernel, n, ny, nz), out_shape=(row, row,...  52 us
    pallas_call x1, Pallas kernels, on_device(): pl.pallas_call(finish, out_shape=(row, row, row, grad, grad), in_specs=[a...  2.61 us

profile of v7, /device:TPU:1, one launch (start us, length us, event | category | flops | bytes accessed | tf_op | source)
XLA Modules:
  0.0 55.3 jit_solution(1335956761698616412)
XLA Ops:
  0.6 52.0 %shard_map.119 = (bf16[6,64,128]{2,1,0:T(8,128)(2,1)}, bf16[6,64,128]{2,1,0:T(8,128)(2,1)}, bf16[6,64,128]{2,1,0:T(8,128)(2,1)}, bf16[4,8,144,128]{3,2,1,0:T(8,128)(2,1)}) custom-call(bf16[6,64,128]{2,1,0:T(8,128)(2,1)} %bitcast.25, bf16[6,64,128]{2,1,0:T(8,128)(2,1)} %bitcast.26, bf16[6,64,128]{2,1,0:T(8,128)(2,1)} %bitcast.27, bf16[1152,128]{1,0:T(8,128)(2,1)} %bitcast.21, ...), custom_call_target="tpu_custom_call" | custom-call | tf_op jit(solution)/shard_map/pallas_call | solution.py:898
  52.7 2.6 %shard_map.120 = (bf16[6,64,128]{2,1,0:T(8,128)(2,1)}, bf16[6,64,128]{2,1,0:T(8,128)(2,1)}, bf16[6,64,128]{2,1,0:T(8,128)(2,1)}, f32[2304,128]{1,0:T(8,128)}, f32[2304,128]{1,0:T(8,128)}) custom-call(bf16[6,64,128]{2,1,0:T(8,128)(2,1)} %get-tuple-element.14.n_ref, bf16[6,64,128]{2,1,0:T(8,128)(2,1)} %get-tuple-element.15.a_ref, ...), custom_call_target="tpu_custom_call" | custom-call | tf_op jit(solution)/shard_map/pallas_call | solution.py:970

commit v8 on v7

--- a/solution.py
+++ b/solution.py
@@ -670,7 +670,6 @@
     first_step(1)
     prepare(1)
     send(1)
-    send_rows(1, (1,))
 
     def p2_copy(d, size):
         q, p = zpeers[d]
@@ -692,6 +691,7 @@
         q, p = ypeers[d]
         return ar("q2", qy.at[q], qyr.at[y], p)
 
+    send_rows(1, (1,))
     arrived("q1", qr.at[pl.ds(0, nz - 1)])
     part = qf[:, z]
     for q, p in zpeers:
@@ -722,6 +722,8 @@
         own_p(size, off).start()
         for d in range(nz - 1):
             p3(d, size, off).start()
+        for q, p in ypeers:
+            ar("p4", fin_p.at[pl.ds(0, size)], out_ref.at[y, z, pl.ds(off, size)], p, y).start()
 
     by_core(stage)
 
@@ -767,7 +769,9 @@
         arrived("p3", out_ref.at[y, pl.ds(0, nz - 1), pl.ds(off, size)])
         own_p(size, off).wait()
         for d in range(ny - 1):
-            p4(d, size, off, True).start()
+            for q, p in zpeers:
+                ref = out_ref.at[y, q, pl.ds(off, size)]
+                ar("p4", ref, ref, ypeers[d][1], y).start()
         cpy_p(y, size, off).start()
 
     by_core(stage)

time: 55.4 us -> 55.7 us (level)
  no operation moved by 1% of the time
where the time goes in v8:
time: 55.7 us; the launch traced here: 55.6 us
  Pallas kernels  55 us (99%)
  between operations  0.64 us (1%)
    pallas_call x1, Pallas kernels, on_device(): pl.pallas_call(functools.partial(kernel, n, ny, nz), out_shape=(row, row,...  52.4 us
    pallas_call x1, Pallas kernels, on_device(): pl.pallas_call(finish, out_shape=(row, row, row, grad, grad), in_specs=[a...  2.61 us

profile of v8, /device:TPU:1, one launch (start us, length us, event | category | flops | bytes accessed | tf_op | source)
XLA Modules:
  0.0 55.6 jit_solution(17496500346604572421)
XLA Ops:
  0.6 52.4 %shard_map.119 = (bf16[6,64,128]{2,1,0:T(8,128)(2,1)}, bf16[6,64,128]{2,1,0:T(8,128)(2,1)}, bf16[6,64,128]{2,1,0:T(8,128)(2,1)}, bf16[4,8,144,128]{3,2,1,0:T(8,128)(2,1)}) custom-call(bf16[6,64,128]{2,1,0:T(8,128)(2,1)} %bitcast.25, bf16[6,64,128]{2,1,0:T(8,128)(2,1)} %bitcast.26, bf16[6,64,128]{2,1,0:T(8,128)(2,1)} %bitcast.27, bf16[1152,128]{1,0:T(8,128)(2,1)} %bitcast.21, ...), custom_call_target="tpu_custom_call" | custom-call | tf_op jit(solution)/shard_map/pallas_call | solution.py:902
  53.0 2.6 %shard_map.120 = (bf16[6,64,128]{2,1,0:T(8,128)(2,1)}, bf16[6,64,128]{2,1,0:T(8,128)(2,1)}, bf16[6,64,128]{2,1,0:T(8,128)(2,1)}, f32[2304,128]{1,0:T(8,128)}, f32[2304,128]{1,0:T(8,128)}) custom-call(bf16[6,64,128]{2,1,0:T(8,128)(2,1)} %get-tuple-element.14.n_ref, bf16[6,64,128]{2,1,0:T(8,128)(2,1)} %get-tuple-element.15.a_ref, ...), custom_call_target="tpu_custom_call" | custom-call | tf_op jit(solution)/shard_map/pallas_call | solution.py:974
